TPU v7x, 256 devices: a whole 4x4x8 slice. The times are simulated.
256 devices in a mesh: dom: 256 (over z, x, y, core).
Axes of the slice: x: 4, y: 4, z: 8, core: 2. Of those that a mesh axis runs over, the one named last changes fastest.
Arguments:
- schur_blocks: float32 [393216, 1536], P('dom'), may hold values from -2 to 5, as said below
- rigid_modes: float32 [1536, 1536], P('dom'), may hold values from -0.15625 to 0.15625
- coarse_inverse: float32 [1536, 1536], P('dom'), may hold values from -1 to 3, as said below
- local_gaps: float32 [32, 393216], P(None, 'dom'), may hold values from -8 to 8
- glue_peer: int32 [256, 6], P('dom'), may hold values from -1 to 255, as said below
- glue_offset: int32 [256, 6], P('dom'), may hold values from 0 to 11, as said below
- glue_count: int32 [256, 6], P('dom'), may hold values from 0 to 2, as said below
- glue_sign: int32 [256, 6], P('dom'), may hold values from -1 to 1, as said below
- mode_counts: int32 [256], P('dom'), may hold values from 0 to 6
Outputs:
- solution: float32 [32, 393216], P(None, 'dom')
- residual: float32 [32, 393216], P(None, 'dom')
Inputs may be any that keep to these rules, and one draw needn't show every extreme that they name: `glue_peer`: subdomains form a grid of 16 x 4 x 4, subdomain (i * 4 + j) * 4 + k at grid place (i, j, k). Each subdomain lists each of its face neighbours in exactly one entry, in an order of its own; the other entries are -1. `glue_count`: zero exactly where the entry is -1; the same on both sides of a pair. The ranges of one subdomain's entries do not intersect. glue_offset + glue_count <= 12; 11 where the entry is -1. The m-th row of a shared range on one side is glued to the m-th row of the range on the other side. `glue_sign`: opposite on the two sides of a pair; 0 exactly where the entry is -1. `schur_blocks`: each subdomain's block is symmetric positive definite. `coarse_inverse`: Symmetric.
All inputs are finite; a program needn't handle non-finite values.
Results may differ from a plain program's by a relative error of at most 0.0003.
Values sent between devices are 32-bit elements; how exact they have to be, the bound alone decides.
No kernel may reach another device: no remote copies, remote signals or barrier semaphores. Data moves between devices by JAX's collectives and lax.ppermute only.
A program may use at most 64 MiB of HBM per device.

v0:
```python
import jax
import jax.numpy as jnp
from jax import lax
from jax.sharding import PartitionSpec as P

BLK = 128
NM = 6
MAXC = 2
GY = 4
GZ = 4
ITERS = 2


def from_behind(block, axis, distance):
    devices = range(lax.axis_size(axis))
    route = [(i - distance, i) for i in devices if i - distance in devices]
    return lax.ppermute(block, axis, route)


def shards(
    schur_blocks,
    rigid_modes,
    coarse_inverse,
    local_gaps,
    glue_peer,
    glue_offset,
    glue_count,
    glue_sign,
    mode_counts,
):
    highest = lax.Precision.HIGHEST
    order_rows = schur_blocks.shape[0]
    window_rows = MAXC * BLK
    my_index = lax.axis_index("dom")
    peer_row = glue_peer[0]
    offset_row = glue_offset[0]
    count_row = glue_count[0]
    sign_row = glue_sign[0]
    row_block = jnp.arange(order_rows, dtype=jnp.int32) // BLK
    inside = (row_block[None, :] >= offset_row[:, None]) & (
        row_block[None, :] < (offset_row + count_row)[:, None]
    )
    row_sign = jnp.sum(jnp.where(inside, sign_row[:, None], 0), axis=0).astype(jnp.float32)
    kept_mode = jnp.arange(NM, dtype=jnp.int32) < mode_counts[0]
    masked_modes = jnp.where(kept_mode[:, None], rigid_modes, 0.0)
    strides = [1, -1, GZ, -GZ, GY * GZ, -GY * GZ]
    window_ids = jnp.arange(window_rows, dtype=jnp.int32)

    def glue_field(field):
        padding = jnp.zeros((field.shape[0], window_rows), jnp.float32)
        padded = jnp.concatenate([field, padding], axis=1)
        total = padded
        for stride in strides:
            to_peer = peer_row == my_index + stride
            send_start = jnp.sum(jnp.where(to_peer, offset_row, 0)) * BLK
            outgoing = lax.dynamic_slice_in_dim(padded, send_start, window_rows, 1)
            incoming = from_behind(outgoing, "dom", stride)
            from_peer = peer_row == my_index - stride
            recv_start = jnp.sum(jnp.where(from_peer, offset_row, 0)) * BLK
            recv_rows = jnp.sum(jnp.where(from_peer, count_row, 0)) * BLK
            masked_in = jnp.where((window_ids < recv_rows)[None, :], incoming, 0.0)
            placed = lax.dynamic_update_slice_in_dim(
                jnp.zeros_like(padded), masked_in, recv_start, 1
            )
            total = total + placed
        return total[:, :order_rows]

    def coarse_coeffs(weights):
        term = jnp.dot(
            weights, coarse_inverse, precision=highest, preferred_element_type=jnp.float32
        )
        whole = lax.psum(term, "dom")
        return (lax.dynamic_slice_in_dim(whole, my_index * NM, NM, 1), whole)

    def glue_lifted(own_coeffs):
        lifted = row_sign * jnp.dot(
            own_coeffs, masked_modes, precision=highest, preferred_element_type=jnp.float32
        )
        return glue_field(lifted)

    def project(field):
        weights = lax.dot_general(
            row_sign * field,
            masked_modes,
            (((1,), (1,)), ((), ())),
            precision=highest,
            preferred_element_type=jnp.float32,
        )
        own_coeffs, whole = coarse_coeffs(weights)
        return field - glue_lifted(own_coeffs)

    def inner_product(first_field, second_field):
        return lax.dot_general(
            first_field,
            second_field,
            (((1,), (1,)), ((), ())),
            precision=highest,
            preferred_element_type=jnp.float32,
        )

    def gram_solve(matrix, target):
        return jax.scipy.linalg.cho_solve((jnp.linalg.cholesky(matrix), True), target)

    dual_rhs = glue_field(row_sign * local_gaps)
    residual = project(dual_rhs)
    direction = residual
    solution = jnp.zeros_like(residual)
    res_gram = lax.psum(inner_product(residual, residual), "dom")
    for iteration in range(ITERS):
        projected = project(direction)
        product = jnp.dot(
            row_sign * projected,
            schur_blocks,
            precision=highest,
            preferred_element_type=jnp.float32,
        )
        schur_image = glue_field(row_sign * product)
        proj_image = project(schur_image)
        curvature = lax.psum(inner_product(projected, schur_image), "dom")
        steplen = gram_solve(curvature, res_gram)
        solution = solution + jnp.dot(
            steplen.T, direction, precision=highest, preferred_element_type=jnp.float32
        )
        residual = residual - jnp.dot(
            steplen.T, proj_image, precision=highest, preferred_element_type=jnp.float32
        )
        new_gram = lax.psum(inner_product(residual, residual), "dom")
        beta_coef = gram_solve(res_gram, new_gram)
        direction = residual + jnp.dot(
            beta_coef.T, direction, precision=highest, preferred_element_type=jnp.float32
        )
        res_gram = new_gram
    return (solution, residual)


def solution(mesh):
    return jax.shard_map(
        shards,
        mesh=mesh,
        in_specs=(
            P("dom", None),
            P("dom", None),
            P("dom", None),
            P(None, "dom"),
            P("dom", None),
            P("dom", None),
            P("dom", None),
            P("dom", None),
            P("dom"),
        ),
        out_specs=(P(None, "dom"), P(None, "dom")),
        check_vma=False,
    )
```

profile of v0, /device:TPU:1, one launch (start us, length us, event | category | flops | bytes accessed | tf_op | source)
XLA Modules:
  0.0 1784.6 jit_solution(11973346429729642187)
XLA Ops:
  11.3 4.6 collective-permute-start
  26.8 4.5 collective-permute-start.2
  32.7 7.4 collective-permute-start.4
  43.3 256.7 %all-reduce.15.cloned.1.call-done = f32[32,1536]{1,0:T(8,128)} async-done(((f32[32,1536]{1,0:T(8,128)}), f32[32,1536]{1,0:T(8,128)}) %all-reduce.15.cloned.1.call-update) | async-done | bytes 196624 | tf_op jit(solution)/shard_map/psum | solution.py:72
  301.2 3.6 collective-permute-start.6
  309.1 5.8 collective-permute-start.8
  316.2 9.1 collective-permute-start.10
  328.6 251.0 %all-reduce.17.cloned.1.call-done = f32[32,1536]{1,0:T(8,128)} async-done(((f32[32,1536]{1,0:T(8,128)}), f32[32,1536]{1,0:T(8,128)}) %all-reduce.17.cloned.1.call-update) | async-done | bytes 196624 | tf_op jit(solution)/shard_map/psum | solution.py:72
  580.8 3.6 collective-permute-start.12
  588.7 5.8 collective-permute-start.14
  595.8 9.1 collective-permute-start.16
  606.0 7.9 convolution_multiply_fusion.4
  621.3 5.6 collective-permute-start.20
  628.2 14.5 collective-permute-start.22
  644.4 87.1 %all-reduce.8 = (f32[32,32]{0,1:T(8,128)S(1)}, f32[32,32]{0,1:T(8,128)S(1)}) all-reduce(f32[32,32]{0,1:T(8,128)S(1)} %fusion.103, f32[32,32]{0,1:T(8,128)S(1)} %fusion.19), channel_id=1, replica_groups=mesh['dom'=256] {'dom'}, use_global_device_ids=true, to_apply=%region_18.20 | all-reduce | flops 2048 | bytes 16384 | tf_op jit(solution)/shard_map/psum | solution.py:108
  742.7 244.6 %all-reduce.19.cloned.1.call-done = f32[32,1536]{1,0:T(8,128)} async-done(((f32[32,1536]{1,0:T(8,128)}), f32[32,1536]{1,0:T(8,128)}) %all-reduce.19.cloned.1.call-update) | async-done | bytes 196624 | tf_op jit(solution)/shard_map/psum | solution.py:72
  988.5 3.6 collective-permute-start.24
  999.5 5.8 collective-permute-start.26
  1006.6 9.1 collective-permute-start.28
  1017.4 81.0 %psum.68 = f32[32,32]{1,0:T(8,128)S(1)} all-reduce(f32[32,32]{1,0:T(8,128)S(1)} %fusion.106), channel_id=1, replica_groups=mesh['dom'=256] {'dom'}, use_global_device_ids=true, to_apply=%region_20.23 | all-reduce | flops 1024 | bytes 8192 | tf_op jit(solution)/shard_map/psum | solution.py:127
  1100.5 244.7 %all-reduce.21.cloned.1.call-done = f32[32,1536]{1,0:T(8,128)} async-done(((f32[32,1536]{1,0:T(8,128)}), f32[32,1536]{1,0:T(8,128)}) %all-reduce.21.cloned.1.call-update) | async-done | bytes 196624 | tf_op jit(solution)/shard_map/psum | solution.py:72
  1346.3 3.6 collective-permute-start.30
  1354.2 5.8 collective-permute-start.32
  1361.4 9.1 collective-permute-start.34
  1371.5 7.9 convolution_multiply_fusion.1
  1386.9 5.6 collective-permute-start.38
  1393.8 14.5 collective-permute-start.40
  1410.0 87.0 %psum.70 = f32[32,32]{0,1:T(8,128)S(1)} all-reduce(f32[32,32]{0,1:T(8,128)S(1)} %fusion.15), channel_id=1, replica_groups=mesh['dom'=256] {'dom'}, use_global_device_ids=true, to_apply=%region_22.25 | all-reduce | flops 1024 | bytes 8192 | tf_op jit(solution)/shard_map/psum | solution.py:119
  1505.0 244.7 %all-reduce.23.cloned.1.call-done = f32[32,1536]{1,0:T(8,128)} async-done(((f32[32,1536]{1,0:T(8,128)}), f32[32,1536]{1,0:T(8,128)}) %all-reduce.23.cloned.1.call-update) | async-done | bytes 196624 | tf_op jit(solution)/shard_map/psum | solution.py:72
  1750.9 3.6 collective-permute-start.42
  1759.7 5.8 collective-permute-start.44
  1766.9 9.1 collective-permute-start.46
  (215 shorter events, 99.6 us)
Async XLA Ops:
  7.2 292.9 %all-reduce.15.cloned.1.call-start = ((), (), s32[]{:S(2)}) async-start(), calls=%async_computation | async-start | bytes 393216 | tf_op jit(solution)/shard_map/psum | solution.py:72
  23.6 16.4 collective-permute-start.1
  25.5 15.5 collective-permute-start.5
  43.3 536.4 %all-reduce.17.cloned.1.call-start = ((), (), s32[]{:S(2)}) async-start(), calls=%async_computation.1 | async-start | bytes 393216 | tf_op jit(solution)/shard_map/psum | solution.py:72
  305.9 19.5 %collective-permute-start.7 = (f32[32,256]{1,0:T(8,128)S(1)}, f32[32,256]{1,0:T(8,128)S(1)}, u32[]{:S(2)}, u32[]{:S(2)}) collective-permute-start(f32[32,256]{1,0:T(8,128)S(1)} %get-tuple-element.62), channel_id=1, source_target_pairs={{1,0},{2,1},{3,2},{4,3},{5,4},{6,5},{7,6},{8,7},{9,8},{10,9},{11,1... | collective-permute-start | bytes 98312 | tf_op jit(solution)/shard_map/ppermute | solution.py:17
  307.8 18.6 %collective-permute-start.11 = (f32[32,256]{1,0:T(8,128)S(1)}, f32[32,256]{1,0:T(8,128)S(1)}, u32[]{:S(2)}, u32[]{:S(2)}) collective-permute-start(f32[32,256]{1,0:T(8,128)S(1)} %get-tuple-element.60), channel_id=1, source_target_pairs={{16,0},{17,1},{18,2},{19,3},{20,4},{21,5},{22,6},{23,7},{24,8},{25... | collective-permute-start | bytes 98312 | tf_op jit(solution)/shard_map/ppermute | solution.py:17
  309.1 16.3 collective-permute-start.8
  328.6 658.8 %all-reduce.19.cloned.1.call-start = ((), (), s32[]{:S(2)}) async-start(), calls=%async_computation.2 | async-start | bytes 393216 | tf_op jit(solution)/shard_map/psum | solution.py:72
  585.4 19.5 %collective-permute-start.13 = (f32[32,256]{1,0:T(8,128)S(1)}, f32[32,256]{1,0:T(8,128)S(1)}, u32[]{:S(2)}, u32[]{:S(2)}) collective-permute-start(f32[32,256]{1,0:T(8,128)S(1)} %get-tuple-element.56), channel_id=1, source_target_pairs={{1,0},{2,1},{3,2},{4,3},{5,4},{6,5},{7,6},{8,7},{9,8},{10,9},{11,1... | collective-permute-start | bytes 98312 | tf_op jit(solution)/shard_map/ppermute | solution.py:17
  587.4 18.6 %collective-permute-start.17 = (f32[32,256]{1,0:T(8,128)S(1)}, f32[32,256]{1,0:T(8,128)S(1)}, u32[]{:S(2)}, u32[]{:S(2)}) collective-permute-start(f32[32,256]{1,0:T(8,128)S(1)} %get-tuple-element.54), channel_id=1, source_target_pairs={{16,0},{17,1},{18,2},{19,3},{20,4},{21,5},{22,6},{23,7},{24,8},{25... | collective-permute-start | bytes 98312 | tf_op jit(solution)/shard_map/ppermute | solution.py:17
  588.7 16.3 collective-permute-start.14
  617.8 24.9 %collective-permute-start.19 = (f32[32,256]{1,0:T(8,128)S(1)}, f32[32,256]{1,0:T(8,128)S(1)}, u32[]{:S(2)}, u32[]{:S(2)}) collective-permute-start(f32[32,256]{1,0:T(8,128)S(1)} %get-tuple-element.50), channel_id=1, source_target_pairs={{1,0},{2,1},{3,2},{4,3},{5,4},{6,5},{7,6},{8,7},{9,8},{10,9},{11,1... | collective-permute-start | bytes 98312 | tf_op jit(solution)/shard_map/ppermute | solution.py:17
  620.0 23.7 %collective-permute-start.23 = (f32[32,256]{1,0:T(8,128)S(1)}, f32[32,256]{1,0:T(8,128)S(1)}, u32[]{:S(2)}, u32[]{:S(2)}) collective-permute-start(f32[32,256]{1,0:T(8,128)S(1)} %get-tuple-element.48), channel_id=1, source_target_pairs={{16,0},{17,1},{18,2},{19,3},{20,4},{21,5},{22,6},{23,7},{24,8},{25... | collective-permute-start | bytes 98312 | tf_op jit(solution)/shard_map/ppermute | solution.py:17
  621.3 21.4 %collective-permute-start.20 = (f32[32,256]{1,0:T(8,128)S(1)}, f32[32,256]{1,0:T(8,128)S(1)}, u32[]{:S(2)}, u32[]{:S(2)}) collective-permute-start(f32[32,256]{1,0:T(8,128)S(1)} %get-tuple-element.51), channel_id=1, source_target_pairs={{0,4},{1,5},{2,6},{3,7},{4,8},{5,9},{6,10},{7,11},{8,12},{9,13},{1... | collective-permute-start | bytes 98312 | tf_op jit(solution)/shard_map/ppermute | solution.py:17
  626.9 15.9 collective-permute-start.21
  628.2 15.5 collective-permute-start.22
  742.7 602.5 %all-reduce.21.cloned.1.call-start = ((), (), s32[]{:S(2)}) async-start(), calls=%async_computation.3 | async-start | bytes 393216 | tf_op jit(solution)/shard_map/psum | solution.py:72
  993.1 22.6 %collective-permute-start.25 = (f32[32,256]{1,0:T(8,128)S(1)}, f32[32,256]{1,0:T(8,128)S(1)}, u32[]{:S(2)}, u32[]{:S(2)}) collective-permute-start(f32[32,256]{1,0:T(8,128)S(1)} %get-tuple-element.44), channel_id=1, source_target_pairs={{1,0},{2,1},{3,2},{4,3},{5,4},{6,5},{7,6},{8,7},{9,8},{10,9},{11,1... | collective-permute-start | bytes 98312 | tf_op jit(solution)/shard_map/ppermute | solution.py:17
  998.2 18.6 %collective-permute-start.29 = (f32[32,256]{1,0:T(8,128)S(1)}, f32[32,256]{1,0:T(8,128)S(1)}, u32[]{:S(2)}, u32[]{:S(2)}) collective-permute-start(f32[32,256]{1,0:T(8,128)S(1)} %get-tuple-element.42), channel_id=1, source_target_pairs={{16,0},{17,1},{18,2},{19,3},{20,4},{21,5},{22,6},{23,7},{24,8},{25... | collective-permute-start | bytes 98312 | tf_op jit(solution)/shard_map/ppermute | solution.py:17
  999.5 16.3 collective-permute-start.26
  1100.5 649.2 %all-reduce.23.cloned.1.call-start = ((), (), s32[]{:S(2)}) async-start(), calls=%async_computation.4 | async-start | bytes 393216 | tf_op jit(solution)/shard_map/psum | solution.py:72
  1351.0 19.5 %collective-permute-start.31 = (f32[32,256]{1,0:T(8,128)S(1)}, f32[32,256]{1,0:T(8,128)S(1)}, u32[]{:S(2)}, u32[]{:S(2)}) collective-permute-start(f32[32,256]{1,0:T(8,128)S(1)} %get-tuple-element.38), channel_id=1, source_target_pairs={{1,0},{2,1},{3,2},{4,3},{5,4},{6,5},{7,6},{8,7},{9,8},{10,9},{11,1... | collective-permute-start | bytes 98312 | tf_op jit(solution)/shard_map/ppermute | solution.py:17
  1352.9 18.6 %collective-permute-start.35 = (f32[32,256]{1,0:T(8,128)S(1)}, f32[32,256]{1,0:T(8,128)S(1)}, u32[]{:S(2)}, u32[]{:S(2)}) collective-permute-start(f32[32,256]{1,0:T(8,128)S(1)} %get-tuple-element.36), channel_id=1, source_target_pairs={{16,0},{17,1},{18,2},{19,3},{20,4},{21,5},{22,6},{23,7},{24,8},{25... | collective-permute-start | bytes 98312 | tf_op jit(solution)/shard_map/ppermute | solution.py:17
  1354.2 16.3 collective-permute-start.32
  1383.3 25.0 %collective-permute-start.37 = (f32[32,256]{1,0:T(8,128)S(1)}, f32[32,256]{1,0:T(8,128)S(1)}, u32[]{:S(2)}, u32[]{:S(2)}) collective-permute-start(f32[32,256]{1,0:T(8,128)S(1)} %get-tuple-element.32), channel_id=1, source_target_pairs={{1,0},{2,1},{3,2},{4,3},{5,4},{6,5},{7,6},{8,7},{9,8},{10,9},{11,1... | collective-permute-start | bytes 98312 | tf_op jit(solution)/shard_map/ppermute | solution.py:17
  1385.6 23.7 %collective-permute-start.41 = (f32[32,256]{1,0:T(8,128)S(1)}, f32[32,256]{1,0:T(8,128)S(1)}, u32[]{:S(2)}, u32[]{:S(2)}) collective-permute-start(f32[32,256]{1,0:T(8,128)S(1)} %get-tuple-element.30), channel_id=1, source_target_pairs={{16,0},{17,1},{18,2},{19,3},{20,4},{21,5},{22,6},{23,7},{24,8},{25... | collective-permute-start | bytes 98312 | tf_op jit(solution)/shard_map/ppermute | solution.py:17
  1386.9 21.4 %collective-permute-start.38 = (f32[32,256]{1,0:T(8,128)S(1)}, f32[32,256]{1,0:T(8,128)S(1)}, u32[]{:S(2)}, u32[]{:S(2)}) collective-permute-start(f32[32,256]{1,0:T(8,128)S(1)} %get-tuple-element.33), channel_id=1, source_target_pairs={{0,4},{1,5},{2,6},{3,7},{4,8},{5,9},{6,10},{7,11},{8,12},{9,13},{1... | collective-permute-start | bytes 98312 | tf_op jit(solution)/shard_map/ppermute | solution.py:17
  1392.5 15.9 collective-permute-start.39
  1393.8 15.5 collective-permute-start.40
  1755.5 20.5 %collective-permute-start.43 = (f32[32,256]{1,0:T(8,128)S(1)}, f32[32,256]{1,0:T(8,128)S(1)}, u32[]{:S(2)}, u32[]{:S(2)}) collective-permute-start(f32[32,256]{1,0:T(8,128)S(1)} %get-tuple-element.26), channel_id=1, source_target_pairs={{1,0},{2,1},{3,2},{4,3},{5,4},{6,5},{7,6},{8,7},{9,8},{10,9},{11,1... | collective-permute-start | bytes 98312 | tf_op jit(solution)/shard_map/ppermute | solution.py:17
  1758.4 18.6 %collective-permute-start.47 = (f32[32,256]{1,0:T(8,128)S(1)}, f32[32,256]{1,0:T(8,128)S(1)}, u32[]{:S(2)}, u32[]{:S(2)}) collective-permute-start(f32[32,256]{1,0:T(8,128)S(1)} %get-tuple-element.24), channel_id=1, source_target_pairs={{16,0},{17,1},{18,2},{19,3},{20,4},{21,5},{22,6},{23,7},{24,8},{25... | collective-permute-start | bytes 98312 | tf_op jit(solution)/shard_map/ppermute | solution.py:17
  1759.7 16.3 collective-permute-start.44
  (23 other events, 815.3 us)
Sparse Core Ops, SparseCore 0:
  43.4 256.6 all-reduce.14
  328.7 250.8 all-reduce.16
  742.8 244.5 all-reduce.18
  1100.6 244.5 all-reduce.20
  1504.9 244.7 all-reduce.22
where the time goes:
time: 1790 us; the launch traced here: 1780 us
  waiting for transfers between devices  1260 us (70%)
  blocking collectives  255 us (14%)
  starting transfers between devices  191 us (11%)
  matrix products  35.2 us (2%)
  other arithmetic  24.2 us (1%)
  between operations  23.3 us (1%)
    psum x5, waiting for transfers between devices, coarse_coeffs(): whole = lax.psum(term, 'dom')  1240 us
    ppermute x48, starting transfers between devices, from_behind(): return lax.ppermute(block, axis, route)  191 us
    psum x1, blocking collectives, shards(): res_gram = lax.psum(inner_product(residual, residual), 'dom')  87.1 us
    psum x1, blocking collectives, shards(): curvature = lax.psum(inner_product(projected, schur_image), 'dom')  87 us
    psum x1, blocking collectives, shards(): new_gram = lax.psum(inner_product(residual, residual), 'dom')  81 us
  transfers between devices with their start and end apart: 53, of which 20 were waited for; matrix products, arithmetic and copies ran while one was open for 0% of the time, Pallas kernels for 0%

commit v1 on v0

v1 whole, which is shorter than its diff:
```python
import jax
import jax.numpy as jnp
from jax import lax
from jax.sharding import PartitionSpec as P

BLK = 128
NB = 12
NM = 6
PM = 8
CASES = 32
MAXC = 2
WIN = MAXC * BLK
GX = 16
GY = 4
GZ = 4
PLANE = GY * GZ
N = GX * PLANE
STEPS = ((0, 0, 1), (0, 0, -1), (0, 1, 0), (0, -1, 0), (1, 0, 0), (-1, 0, 0))
STRIDES = tuple(a * PLANE + b * GZ + c for a, b, c in STEPS)
HIGHEST = lax.Precision.HIGHEST


def route(step):
    pairs = []
    for s in range(N):
        place = (s // PLANE, s // GZ % GY, s % GZ)
        moved = [p + d for p, d in zip(place, step)]
        if all(0 <= m < size for m, size in zip(moved, (GX, GY, GZ))):
            pairs.append((s, (moved[0] * GY + moved[1]) * GZ + moved[2]))
    return pairs


ROUTES = [route(step) for step in STEPS]
IN_PLANE = [[a * PLANE + b for b in range(PLANE)] for a in range(GX)]
ACROSS = [[a * PLANE + b for a in range(GX)] for b in range(PLANE)]


def dot(a, b, precision=HIGHEST):
    return jnp.dot(a, b, precision=precision, preferred_element_type=jnp.float32)


def dot_t(a, b):
    return lax.dot_general(
        a, b, (((1,), (1,)), ((), ())), precision=HIGHEST, preferred_element_type=jnp.float32
    )


def gram_solve(matrix, target):
    return jax.scipy.linalg.cho_solve((jnp.linalg.cholesky(matrix), True), target)


def swap(block, groups):
    return lax.all_to_all(block, "dom", 0, 0, tiled=True, axis_index_groups=groups)


def shift(stack, by, axis):
    if by == 0:
        return stack
    pad = [(0, 0)] * stack.ndim
    pad[axis] = (max(by, 0), max(-by, 0))
    padded = jnp.pad(stack, pad)
    start = max(-by, 0)
    return lax.slice_in_dim(padded, start, start + stack.shape[axis], axis=axis)


def shards(
    schur_blocks,
    rigid_modes,
    coarse_inverse,
    local_gaps,
    glue_peer,
    glue_offset,
    glue_count,
    glue_sign,
    mode_counts,
):
    rows = schur_blocks.shape[0]
    me = lax.axis_index("dom")
    peer, offset, count, sign = glue_peer[0], glue_offset[0], glue_count[0], glue_sign[0]
    block_id = jnp.arange(rows, dtype=jnp.int32) // BLK
    inside = (block_id[None, :] >= offset[:, None]) & (
        block_id[None, :] < (offset + count)[:, None]
    )
    row_sign = jnp.sum(jnp.where(inside, sign[:, None], 0), axis=0).astype(jnp.float32)
    window_id = jnp.arange(WIN, dtype=jnp.int32)
    starts, sizes = [], []
    for stride in STRIDES:
        hit = (peer == me + stride) & (count > 0)
        starts.append(jnp.sum(jnp.where(hit, offset, 0)) * BLK)
        sizes.append(jnp.sum(jnp.where(hit, count, 0)) * BLK)

    def faces(field):
        padded = jnp.pad(field, ((0, 0), (0, WIN)))
        out = [None] * 6
        for d in range(6):
            window = lax.dynamic_slice_in_dim(padded, starts[d], WIN, 1)
            got = lax.ppermute(window, "dom", ROUTES[d])
            out[d ^ 1] = got
        return [
            jnp.where((window_id < sizes[d])[None, :], out[d], 0.0) for d in range(6)
        ]

    def place(face, d):
        zero = jnp.zeros((face.shape[0], rows + WIN), jnp.float32)
        return lax.dynamic_update_slice_in_dim(zero, face, starts[d], 1)[:, :rows]

    def assemble(field, got):
        total = field
        for d in range(6):
            total = total + place(got[d], d)
        return total

    kept = jnp.arange(PM, dtype=jnp.int32) < mode_counts[0]
    modes = jnp.where(kept[:, None], jnp.pad(rigid_modes, ((0, PM - NM), (0, 0))), 0.0) * row_sign

    gaps = row_sign * local_gaps
    got = faces(jnp.concatenate([gaps, modes], axis=0))
    dual_rhs = assemble(gaps, [g[:CASES] for g in got])
    lifts = jnp.concatenate([modes] + [place(got[d][CASES:], d) for d in range(6)], axis=0)

    own_rows = jnp.pad(coarse_inverse.reshape(NM, N, NM), ((0, PM - NM), (0, 0), (0, PM - NM)))
    own_rows = own_rows.reshape(PM, N * 2, 4).transpose(2, 0, 1)
    near = [own_rows]
    for d in range(6):
        near.append(lax.ppermute(own_rows, "dom", ROUTES[d ^ 1]))
    coarse = jnp.stack(near, axis=1).reshape(4 * 7 * PM, N * 2)

    def apply_coarse(gathered):
        full = dot(coarse, gathered.reshape(N * 2, 128)).reshape(4, 7 * PM, 4, CASES)
        return full[0, :, 0] + full[1, :, 1] + full[2, :, 2] + full[3, :, 3]

    def gather(weights):
        chunk = weights.reshape(1, 2, 128)
        return swap(jnp.broadcast_to(chunk, (N, 2, 128)), None)

    def lift(coeffs):
        return lax.dot_general(
            coeffs, lifts, (((0,), (0,)), ((), ())), precision=HIGHEST,
            preferred_element_type=jnp.float32,
        )

    def gather_sum(weights, *grams):
        part = jnp.concatenate([weights.reshape(1, 2, 128)] + [g.reshape(1, 8, 128) for g in grams], 1)
        first = swap(jnp.broadcast_to(part, (PLANE,) + part.shape[1:]), IN_PLANE)
        sums = jnp.sum(first[:, 2:], axis=0, keepdims=True)
        part = jnp.concatenate([first[:, :2].reshape(1, 2 * PLANE, 128), sums], 1)
        second = swap(jnp.broadcast_to(part, (GX,) + part.shape[1:]), ACROSS)
        totals = jnp.sum(second[:, 2 * PLANE:], axis=0).reshape(len(grams), CASES, CASES)
        return second[:, : 2 * PLANE].reshape(N, 2, 128), totals

    def gather_terms(terms, *grams):
        part = jnp.concatenate([terms.reshape(1, 14, 128)] + [g.reshape(1, 8, 128) for g in grams], 1)
        first = swap(jnp.broadcast_to(part, (PLANE,) + part.shape[1:]), IN_PLANE)
        sums = jnp.sum(first[:, 14:], axis=0, keepdims=True)
        by_dir = first[:, :14].reshape(PLANE, 7, 2, 128)
        plane = by_dir[:, 0]
        for d in range(4):
            plane = plane + shift(by_dir[:, d + 1], STRIDES[d], 0)
        part = jnp.stack([plane, by_dir[:, 5], by_dir[:, 6]], 0).reshape(1, 6 * PLANE, 128)
        part = jnp.concatenate([part, sums], 1)
        second = swap(jnp.broadcast_to(part, (GX,) + part.shape[1:]), ACROSS)
        totals = jnp.sum(second[:, 6 * PLANE:], axis=0).reshape(len(grams), CASES, CASES)
        three = second[:, : 6 * PLANE].reshape(GX, 3, 2 * PLANE, 128)
        whole = three[:, 0] + shift(three[:, 1], 1, 0) + shift(three[:, 2], -1, 0)
        return whole.reshape(N, 2, 128), totals

    def local_schur(field):
        return row_sign * dot(row_sign * field, schur_blocks)

    coeffs = apply_coarse(gather(dot_t(modes, dual_rhs)))
    residual = dual_rhs - lift(coeffs)
    gram_term = dot_t(residual, residual)

    coeffs = apply_coarse(gather(dot_t(modes, residual)))
    projected = residual - lift(coeffs)
    image = local_schur(projected)
    got = faces(image)
    whole, totals = gather_terms(dot_t(lifts, image), 2.0 * dot_t(projected, image), gram_term)
    curvature, res_gram = totals[0], totals[1]
    steplen = gram_solve(curvature, res_gram)
    proj_image = assemble(image, got) - lift(apply_coarse(whole))
    direction = residual
    solution = dot(steplen.T, direction)
    residual = residual - dot(steplen.T, proj_image)

    whole, totals = gather_sum(dot_t(modes, residual), dot_t(residual, residual))
    new_gram = totals[0]
    beta_coef = gram_solve(res_gram, new_gram)
    direction = residual + dot(beta_coef.T, direction)
    projected = residual - lift(apply_coarse(whole)) + dot(beta_coef.T, projected)
    image = local_schur(projected)
    got = faces(image)
    whole, totals = gather_terms(dot_t(lifts, image), 2.0 * dot_t(projected, image))
    steplen = gram_solve(totals[0], new_gram)
    proj_image = assemble(image, got) - lift(apply_coarse(whole))
    solution = solution + dot(steplen.T, direction)
    residual = residual - dot(steplen.T, proj_image)
    return (solution, residual)


def solution(mesh):
    return jax.shard_map(
        shards,
        mesh=mesh,
        in_specs=(
            P("dom", None),
            P("dom", None),
            P("dom", None),
            P(None, "dom"),
            P("dom", None),
            P("dom", None),
            P("dom", None),
            P("dom", None),
            P("dom"),
        ),
        out_specs=(P(None, "dom"), P(None, "dom")),
        check_vma=False,
    )
```

time: 1790 us -> 298 us (0.17)
  waiting for transfers between devices: 1260 us -> 69.3 us
  blocking collectives: 255 us -> 10.7 us
  starting transfers between devices: 191 us -> 130 us
    psum x5 -> x0, waiting for transfers between devices: 1240 us -> none  [coarse_coeffs(): whole = lax.psum(term, 'dom')]
    psum x3 -> x0, blocking collectives: 255 us -> none  [the longest x1 87.1 us: shards(): res_gram = lax.psum(inner_product(residual, residual), 'dom')]
    ppermute x48 -> x24, starting transfers between devices: 191 us -> 70.8 us  [the longest x18 50.9 us: faces(): got = lax.ppermute(window, 'dom', ROUTES[d])]
    all_to_all x0 -> x7, starting transfers between devices: none -> 59.4 us  [swap(): lax.all_to_all(block, 'dom', 0, 0, tiled=True, axis_index_groups=groups)]
    all_to_all x0 -> x7, waiting for transfers between devices: none -> 47.7 us  [swap(): lax.all_to_all(block, 'dom', 0, 0, tiled=True, axis_index_groups=groups)]
  transfers between devices with their start and end apart: 53 -> 31, of which waited for: 20 -> 15; matrix products, arithmetic and copies ran while one was open for 0% -> 6% of each run, Pallas kernels for 0% -> 0%
where the time goes in v1:
time: 298 us; the launch traced here: 293 us
  starting transfers between devices  130 us (44%)
  waiting for transfers between devices  69.3 us (23%)
  matrix products  33.2 us (11%)
  other arithmetic  25.5 us (9%)
  local copies, waits for them, and re-layouts  13.5 us (5%)
  blocking collectives  10.7 us (4%)
  between operations  10.4 us (3%)
    all_to_all x7, starting transfers between devices, swap(): lax.all_to_all(block, 'dom', 0, 0, tiled=True, axis_index_groups=groups)  59.4 us
    ppermute x18, starting transfers between devices, faces(): got = lax.ppermute(window, 'dom', ROUTES[d])  50.9 us
    all_to_all x7, waiting for transfers between devices, swap(): lax.all_to_all(block, 'dom', 0, 0, tiled=True, axis_index_groups=groups)  47.7 us
    dot_general x13, matrix products, dot(): jnp.dot(a, b, precision=precision, preferred_element_type=jnp.float32)  27.9 us
    ppermute x18, waiting for transfers between devices, faces(): got = lax.ppermute(window, 'dom', ROUTES[d])  20.2 us
    ppermute x6, starting transfers between devices, shards(): near.append(lax.ppermute(own_rows, 'dom', ROUTES[d ^ 1]))  19.9 us
    another operation x9, other arithmetic, gram_solve(): jnp.linalg.cholesky(matrix)  10.8 us
    all_to_all x1, blocking collectives, swap(): lax.all_to_all(block, 'dom', 0, 0, tiled=True, axis_index_groups=groups)  10.7 us
  transfers between devices with their start and end apart: 31, of which 15 were waited for; matrix products, arithmetic and copies ran while one was open for 6% of the time, Pallas kernels for 0%

profile of v1, /device:TPU:1, one launch (start us, length us, event | category | flops | bytes accessed | tf_op | source)
XLA Modules:
  0.0 292.8 jit_solution(2628312479252346673)
XLA Ops:
  4.3 5.1 %collective-permute-start.6 = (f32[4,8,512]{2,1,0:T(8,128)S(1)}, f32[4,8,512]{2,1,0:T(8,128)S(1)}, u32[]{:S(2)}, u32[]{:S(2)}) collective-permute-start(f32[4,8,512]{2,1,0:T(8,128)S(1)} %copy.102), channel_id=1, source_target_pairs={{1,0},{2,1},{3,2},{5,4},{6,5},{7,6},{9,8},{10,9},{11,10},{13,12},{... | collective-permute-start | bytes 196616 | tf_op jit(solution)/shard_map/ppermute | solution.py:125
  12.7 5.5 %collective-permute-start.9 = (f32[4,8,512]{2,1,0:T(8,128)S(1)}, f32[4,8,512]{2,1,0:T(8,128)S(1)}, u32[]{:S(2)}, u32[]{:S(2)}) collective-permute-start(f32[4,8,512]{2,1,0:T(8,128)S(1)} %copy.102), channel_id=1, source_target_pairs={{0,4},{1,5},{2,6},{3,7},{4,8},{5,9},{6,10},{7,11},{8,12},{9,13},{1... | collective-permute-start | bytes 196616 | tf_op jit(solution)/shard_map/ppermute | solution.py:125
  27.0 3.0 %collective-permute-start = (f32[40,256]{1,0:T(8,128)S(1)}, f32[40,256]{1,0:T(8,128)S(1)}, u32[]{:S(2)}, u32[]{:S(2)}) collective-permute-start(f32[40,256]{1,0:T(8,128)S(1)} %get-tuple-element.22), channel_id=1, source_target_pairs={{1,0},{2,1},{3,2},{5,4},{6,5},{7,6},{9,8},{10,9},{11,10},{13,12},{... | collective-permute-start | bytes 122888 | tf_op jit(solution)/shard_map/ppermute | solution.py:97
  39.2 5.5 %collective-permute-done.2 = f32[40,256]{1,0:T(8,128)S(1)} collective-permute-done((f32[40,256]{1,0:T(8,128)S(1)}, f32[40,256]{1,0:T(8,128)S(1)}, u32[]{:S(2)}, u32[]{:S(2)}) %collective-permute-start.2) | collective-permute-done | bytes 40992 | tf_op jit(solution)/shard_map/ppermute | solution.py:97
  44.7 5.3 %collective-permute-start.3 = (f32[40,256]{1,0:T(8,128)S(1)}, f32[40,256]{1,0:T(8,128)S(1)}, u32[]{:S(2)}, u32[]{:S(2)}) collective-permute-start(f32[40,256]{1,0:T(8,128)S(1)} %get-tuple-element.24), channel_id=1, source_target_pairs={{0,4},{1,5},{2,6},{3,7},{4,8},{5,9},{6,10},{7,11},{8,12},{9,13},{1... | collective-permute-start | bytes 122888 | tf_op jit(solution)/shard_map/ppermute | solution.py:97
  52.6 4.9 %collective-permute-done.4 = f32[40,256]{1,0:T(8,128)S(1)} collective-permute-done((f32[40,256]{1,0:T(8,128)S(1)}, f32[40,256]{1,0:T(8,128)S(1)}, u32[]{:S(2)}, u32[]{:S(2)}) %collective-permute-start.4) | collective-permute-done | bytes 40992 | tf_op jit(solution)/shard_map/ppermute | solution.py:97
  57.4 5.5 %collective-permute-start.5 = (f32[40,256]{1,0:T(8,128)S(1)}, f32[40,256]{1,0:T(8,128)S(1)}, u32[]{:S(2)}, u32[]{:S(2)}) collective-permute-start(f32[40,256]{1,0:T(8,128)S(1)} %get-tuple-element.27), channel_id=1, source_target_pairs={{0,16},{1,17},{2,18},{3,19},{4,20},{5,21},{6,22},{7,23},{8,24},{9,... | collective-permute-start | bytes 122888 | tf_op jit(solution)/shard_map/ppermute | solution.py:97
  66.7 23.2 %all-to-all-start = ((f32[256,2,128]{2,1,0:T(2,128)}), f32[256,2,128]{2,1,0:T(2,128)S(1)}, u32[]{:S(2)}, u32[]{:S(2)}) async-start(f32[256,2,128]{2,1,0:T(2,128)} %broadcast_in_dim.254), calls=%async_computation | async-start | bytes 524288 | tf_op jit(solution)/shard_map/all_to_all | solution.py:53
  89.9 4.8 %collective-permute-start.11 = (f32[4,8,512]{2,1,0:T(8,128)S(1)}, f32[4,8,512]{2,1,0:T(8,128)S(1)}, u32[]{:S(2)}, u32[]{:S(2)}) collective-permute-start(f32[4,8,512]{2,1,0:T(8,128)S(1)} %copy.102), channel_id=1, source_target_pairs={{0,16},{1,17},{2,18},{3,19},{4,20},{5,21},{6,22},{7,23},{8,24},{9,... | collective-permute-start | bytes 196616 | tf_op jit(solution)/shard_map/ppermute | solution.py:125
  96.3 8.7 %all-to-all-done = f32[256,2,128]{2,1,0:T(2,128)S(1)} async-done(((f32[256,2,128]{2,1,0:T(2,128)}), f32[256,2,128]{2,1,0:T(2,128)S(1)}, u32[]{:S(2)}, u32[]{:S(2)}) %all-to-all-start) | async-done | bytes 262176 | tf_op jit(solution)/shard_map/all_to_all | solution.py:53
  107.5 6.9 %all-to-all-start.1 = ((f32[256,2,128]{2,1,0:T(2,128)}), f32[256,2,128]{2,1,0:T(2,128)S(1)}, u32[]{:S(2)}, u32[]{:S(2)}) async-start(f32[256,2,128]{2,1,0:T(2,128)} %broadcast_in_dim.256), calls=%async_computation.1 | async-start | bytes 524288 | tf_op jit(solution)/shard_map/all_to_all | solution.py:53
  114.7 14.9 %all-to-all-done.1 = f32[256,2,128]{2,1,0:T(2,128)S(1)} async-done(((f32[256,2,128]{2,1,0:T(2,128)}), f32[256,2,128]{2,1,0:T(2,128)S(1)}, u32[]{:S(2)}, u32[]{:S(2)}) %all-to-all-start.1) | async-done | bytes 262176 | tf_op jit(solution)/shard_map/all_to_all | solution.py:53
  130.9 7.9 %convolution_multiply_fusion.1 = f32[32,1536]{1,0:T(8,128)S(1)} fusion(f32[1536,1536]{1,0:T(8,128)} %param.12, f32[32,1536]{1,0:T(8,128)S(1)} %convolution_subtract_fusion.3, f32[1536]{0:T(1024)S(1)} %convert_element_type.34), kind=kOutput, calls=%fused_computation.1 | convolution fusion | flops 906067968 | bytes 9836544 | tf_op jit(solution)/shard_map/dot_general | solution.py:39
  139.7 10.7 %all_to_all.40 = f32[16,30,128]{2,1,0:T(8,128)S(1)} all-to-all(f32[16,30,128]{2,1,0:T(8,128)S(1)} %broadcast_in_dim.258), channel_id=1, replica_groups={{0,1,2,3,4,5,6,7,8,9,10,11,12,13,14,15},{16,17,18,19,20,21,22,23,24,25,..., dimensions={0} | all-to-all | bytes 491520 | tf_op jit(solution)/shard_map/all_to_all | solution.py:53
  151.6 3.6 %all-to-all-start.3 = ((f32[16,112,128]{2,1,0:T(8,128)}), f32[16,112,128]{2,1,0:T(8,128)S(1)}, u32[]{:S(2)}, u32[]{:S(2)}) async-start(f32[16,112,128]{2,1,0:T(8,128)} %broadcast_in_dim.261), calls=%async_computation.3 | async-start | bytes 1835008 | tf_op jit(solution)/shard_map/all_to_all | solution.py:53
  155.3 4.7 %collective-permute-start.17 = (f32[32,256]{1,0:T(8,128)S(1)}, f32[32,256]{1,0:T(8,128)S(1)}, u32[]{:S(2)}, u32[]{:S(2)}) collective-permute-start(f32[32,256]{1,0:T(8,128)S(1)} %get-tuple-element.39), channel_id=1, source_target_pairs={{0,16},{1,17},{2,18},{3,19},{4,20},{5,21},{6,22},{7,23},{8,24},{9,... | collective-permute-start | bytes 98312 | tf_op jit(solution)/shard_map/ppermute | solution.py:97
  161.3 3.0 %collective-permute-start.15 = (f32[32,256]{1,0:T(8,128)S(1)}, f32[32,256]{1,0:T(8,128)S(1)}, u32[]{:S(2)}, u32[]{:S(2)}) collective-permute-start(f32[32,256]{1,0:T(8,128)S(1)} %get-tuple-element.37), channel_id=1, source_target_pairs={{0,4},{1,5},{2,6},{3,7},{4,8},{5,9},{6,10},{7,11},{8,12},{9,13},{1... | collective-permute-start | bytes 98312 | tf_op jit(solution)/shard_map/ppermute | solution.py:97
  165.6 4.1 %collective-permute-start.13 = (f32[32,256]{1,0:T(8,128)S(1)}, f32[32,256]{1,0:T(8,128)S(1)}, u32[]{:S(2)}, u32[]{:S(2)}) collective-permute-start(f32[32,256]{1,0:T(8,128)S(1)} %get-tuple-element.35), channel_id=1, source_target_pairs={{0,1},{1,2},{2,3},{4,5},{5,6},{6,7},{8,9},{9,10},{10,11},{12,13},{... | collective-permute-start | bytes 98312 | tf_op jit(solution)/shard_map/ppermute | solution.py:97
  171.9 3.3 %collective-permute-done.12 = f32[32,256]{1,0:T(8,128)S(1)} collective-permute-done((f32[32,256]{1,0:T(8,128)S(1)}, f32[32,256]{1,0:T(8,128)S(1)}, u32[]{:S(2)}, u32[]{:S(2)}) %collective-permute-start.12) | collective-permute-done | bytes 32800 | tf_op jit(solution)/shard_map/ppermute | solution.py:97
  179.6 2.9 cholesky.59
  191.0 8.1 %all-to-all-start.4 = ((f32[16,10,128]{2,1,0:T(8,128)}), f32[16,10,128]{2,1,0:T(8,128)S(1)}, u32[]{:S(2)}, u32[]{:S(2)}) async-start(f32[16,10,128]{2,1,0:T(8,128)} %broadcast_in_dim.270), calls=%async_computation.4 | async-start | bytes 262144 | tf_op jit(solution)/shard_map/all_to_all | solution.py:53
  199.1 6.2 %all-to-all-done.4 = f32[16,10,128]{2,1,0:T(8,128)S(1)} async-done(((f32[16,10,128]{2,1,0:T(8,128)}), f32[16,10,128]{2,1,0:T(8,128)S(1)}, u32[]{:S(2)}, u32[]{:S(2)}) %all-to-all-start.4) | async-done | bytes 81952 | tf_op jit(solution)/shard_map/all_to_all | solution.py:53
  206.1 8.4 %all-to-all-start.5 = ((f32[16,40,128]{2,1,0:T(8,128)}), f32[16,40,128]{2,1,0:T(8,128)S(1)}, u32[]{:S(2)}, u32[]{:S(2)}) async-start(f32[16,40,128]{2,1,0:T(8,128)} %broadcast_in_dim.273), calls=%async_computation.5 | async-start | bytes 655360 | tf_op jit(solution)/shard_map/all_to_all | solution.py:53
  221.2 6.7 %all-to-all-done.5 = f32[16,40,128]{2,1,0:T(8,128)S(1)} async-done(((f32[16,40,128]{2,1,0:T(8,128)}), f32[16,40,128]{2,1,0:T(8,128)S(1)}, u32[]{:S(2)}, u32[]{:S(2)}) %all-to-all-start.5) | async-done | bytes 327712 | tf_op jit(solution)/shard_map/all_to_all | solution.py:53
  230.2 7.9 %convolution_multiply_fusion = f32[32,1536]{1,0:T(8,128)S(1)} fusion(f32[1536,1536]{1,0:T(8,128)} %param.12, f32[32,1536]{1,0:T(8,128)S(1)} %convolution_add_fusion.2, f32[1536]{0:T(1024)S(1)} %convert_element_type.34), kind=kOutput, calls=%fused_computation | convolution fusion | flops 906067968 | bytes 9836544 | tf_op jit(solution)/shard_map/dot_general | solution.py:39
  239.6 5.6 %all-to-all-start.6 = ((f32[16,22,128]{2,1,0:T(8,128)}), f32[16,22,128]{2,1,0:T(8,128)S(1)}, u32[]{:S(2)}, u32[]{:S(2)}) async-start(f32[16,22,128]{2,1,0:T(8,128)} %broadcast_in_dim.275), calls=%async_computation.6 | async-start | bytes 393216 | tf_op jit(solution)/shard_map/all_to_all | solution.py:53
  246.2 5.7 %all-to-all-done.6 = f32[16,22,128]{2,1,0:T(8,128)S(1)} async-done(((f32[16,22,128]{2,1,0:T(8,128)}), f32[16,22,128]{2,1,0:T(8,128)S(1)}, u32[]{:S(2)}, u32[]{:S(2)}) %all-to-all-start.6) | async-done | bytes 180256 | tf_op jit(solution)/shard_map/all_to_all | solution.py:53
  253.1 3.6 %all-to-all-start.7 = ((f32[16,104,128]{2,1,0:T(8,128)}), f32[16,104,128]{2,1,0:T(8,128)S(1)}, u32[]{:S(2)}, u32[]{:S(2)}) async-start(f32[16,104,128]{2,1,0:T(8,128)} %broadcast_in_dim.278), calls=%async_computation.7 | async-start | bytes 1703936 | tf_op jit(solution)/shard_map/all_to_all | solution.py:53
  256.8 4.6 %collective-permute-start.23 = (f32[32,256]{1,0:T(8,128)S(1)}, f32[32,256]{1,0:T(8,128)S(1)}, u32[]{:S(2)}, u32[]{:S(2)}) collective-permute-start(f32[32,256]{1,0:T(8,128)S(1)} %get-tuple-element.33), channel_id=1, source_target_pairs={{0,16},{1,17},{2,18},{3,19},{4,20},{5,21},{6,22},{7,23},{8,24},{9,... | collective-permute-start | bytes 98312 | tf_op jit(solution)/shard_map/ppermute | solution.py:97
  263.8 2.9 collective-permute-start.21
  268.0 3.7 %collective-permute-start.19 = (f32[32,256]{1,0:T(8,128)S(1)}, f32[32,256]{1,0:T(8,128)S(1)}, u32[]{:S(2)}, u32[]{:S(2)}) collective-permute-start(f32[32,256]{1,0:T(8,128)S(1)} %get-tuple-element.29), channel_id=1, source_target_pairs={{0,1},{1,2},{2,3},{4,5},{5,6},{6,7},{8,9},{9,10},{10,11},{12,13},{... | collective-permute-start | bytes 98312 | tf_op jit(solution)/shard_map/ppermute | solution.py:97
  273.9 3.3 %collective-permute-done.18 = f32[32,256]{1,0:T(8,128)S(1)} collective-permute-done((f32[32,256]{1,0:T(8,128)S(1)}, f32[32,256]{1,0:T(8,128)S(1)}, u32[]{:S(2)}, u32[]{:S(2)}) %collective-permute-start.18) | collective-permute-done | bytes 32800 | tf_op jit(solution)/shard_map/ppermute | solution.py:97
  (240 shorter events, 82.2 us)
Async XLA Ops:
  0.6 64.8 %copy-start.2 = (f32[32,1536]{1,0:T(8,128)S(1)}, f32[32,1536]{1,0:T(8,128)}, u32[]{:S(2)}) copy-start(f32[32,1536]{1,0:T(8,128)} %param.15) | copy-start | bytes 589828
  4.3 85.6 %collective-permute-start.6 = (f32[4,8,512]{2,1,0:T(8,128)S(1)}, f32[4,8,512]{2,1,0:T(8,128)S(1)}, u32[]{:S(2)}, u32[]{:S(2)}) collective-permute-start(f32[4,8,512]{2,1,0:T(8,128)S(1)} %copy.102), channel_id=1, source_target_pairs={{1,0},{2,1},{3,2},{5,4},{6,5},{7,6},{9,8},{10,9},{11,10},{13,12},{... | collective-permute-start | bytes 196616 | tf_op jit(solution)/shard_map/ppermute | solution.py:125
  9.5 85.3 %collective-permute-start.7 = (f32[4,8,512]{2,1,0:T(8,128)S(1)}, f32[4,8,512]{2,1,0:T(8,128)S(1)}, u32[]{:S(2)}, u32[]{:S(2)}) collective-permute-start(f32[4,8,512]{2,1,0:T(8,128)S(1)} %copy.102), channel_id=1, source_target_pairs={{0,1},{1,2},{2,3},{4,5},{5,6},{6,7},{8,9},{9,10},{10,11},{12,13},{... | collective-permute-start | bytes 196616 | tf_op jit(solution)/shard_map/ppermute | solution.py:125
  11.4 83.4 %collective-permute-start.8 = (f32[4,8,512]{2,1,0:T(8,128)S(1)}, f32[4,8,512]{2,1,0:T(8,128)S(1)}, u32[]{:S(2)}, u32[]{:S(2)}) collective-permute-start(f32[4,8,512]{2,1,0:T(8,128)S(1)} %copy.102), channel_id=1, source_target_pairs={{4,0},{5,1},{6,2},{7,3},{8,4},{9,5},{10,6},{11,7},{12,8},{13,9},{1... | collective-permute-start | bytes 196616 | tf_op jit(solution)/shard_map/ppermute | solution.py:125
  12.7 82.1 %collective-permute-start.9 = (f32[4,8,512]{2,1,0:T(8,128)S(1)}, f32[4,8,512]{2,1,0:T(8,128)S(1)}, u32[]{:S(2)}, u32[]{:S(2)}) collective-permute-start(f32[4,8,512]{2,1,0:T(8,128)S(1)} %copy.102), channel_id=1, source_target_pairs={{0,4},{1,5},{2,6},{3,7},{4,8},{5,9},{6,10},{7,11},{8,12},{9,13},{1... | collective-permute-start | bytes 196616 | tf_op jit(solution)/shard_map/ppermute | solution.py:125
  27.0 7.1 %collective-permute-start = (f32[40,256]{1,0:T(8,128)S(1)}, f32[40,256]{1,0:T(8,128)S(1)}, u32[]{:S(2)}, u32[]{:S(2)}) collective-permute-start(f32[40,256]{1,0:T(8,128)S(1)} %get-tuple-element.22), channel_id=1, source_target_pairs={{1,0},{2,1},{3,2},{5,4},{6,5},{7,6},{9,8},{10,9},{11,10},{13,12},{... | collective-permute-start | bytes 122888 | tf_op jit(solution)/shard_map/ppermute | solution.py:97
  34.1 3.7 %collective-permute-start.1 = (f32[40,256]{1,0:T(8,128)S(1)}, f32[40,256]{1,0:T(8,128)S(1)}, u32[]{:S(2)}, u32[]{:S(2)}) collective-permute-start(f32[40,256]{1,0:T(8,128)S(1)} %get-tuple-element.26), channel_id=1, source_target_pairs={{0,1},{1,2},{2,3},{4,5},{5,6},{6,7},{8,9},{9,10},{10,11},{12,13},{... | collective-permute-start | bytes 122888 | tf_op jit(solution)/shard_map/ppermute | solution.py:97
  37.8 6.9 %collective-permute-start.2 = (f32[40,256]{1,0:T(8,128)S(1)}, f32[40,256]{1,0:T(8,128)S(1)}, u32[]{:S(2)}, u32[]{:S(2)}) collective-permute-start(f32[40,256]{1,0:T(8,128)S(1)} %get-tuple-element.25), channel_id=1, source_target_pairs={{4,0},{5,1},{6,2},{7,3},{8,4},{9,5},{10,6},{11,7},{12,8},{13,9},{1... | collective-permute-start | bytes 122888 | tf_op jit(solution)/shard_map/ppermute | solution.py:97
  44.7 6.5 %collective-permute-start.3 = (f32[40,256]{1,0:T(8,128)S(1)}, f32[40,256]{1,0:T(8,128)S(1)}, u32[]{:S(2)}, u32[]{:S(2)}) collective-permute-start(f32[40,256]{1,0:T(8,128)S(1)} %get-tuple-element.24), channel_id=1, source_target_pairs={{0,4},{1,5},{2,6},{3,7},{4,8},{5,9},{6,10},{7,11},{8,12},{9,13},{1... | collective-permute-start | bytes 122888 | tf_op jit(solution)/shard_map/ppermute | solution.py:97
  51.2 6.2 %collective-permute-start.4 = (f32[40,256]{1,0:T(8,128)S(1)}, f32[40,256]{1,0:T(8,128)S(1)}, u32[]{:S(2)}, u32[]{:S(2)}) collective-permute-start(f32[40,256]{1,0:T(8,128)S(1)} %get-tuple-element.23), channel_id=1, source_target_pairs={{16,0},{17,1},{18,2},{19,3},{20,4},{21,5},{22,6},{23,7},{24,8},{25... | collective-permute-start | bytes 122888 | tf_op jit(solution)/shard_map/ppermute | solution.py:97
  57.4 6.6 %collective-permute-start.5 = (f32[40,256]{1,0:T(8,128)S(1)}, f32[40,256]{1,0:T(8,128)S(1)}, u32[]{:S(2)}, u32[]{:S(2)}) collective-permute-start(f32[40,256]{1,0:T(8,128)S(1)} %get-tuple-element.27), channel_id=1, source_target_pairs={{0,16},{1,17},{2,18},{3,19},{4,20},{5,21},{6,22},{7,23},{8,24},{9,... | collective-permute-start | bytes 122888 | tf_op jit(solution)/shard_map/ppermute | solution.py:97
  64.1 30.8 %collective-permute-start.10 = (f32[4,8,512]{2,1,0:T(8,128)S(1)}, f32[4,8,512]{2,1,0:T(8,128)S(1)}, u32[]{:S(2)}, u32[]{:S(2)}) collective-permute-start(f32[4,8,512]{2,1,0:T(8,128)S(1)} %copy.102), channel_id=1, source_target_pairs={{16,0},{17,1},{18,2},{19,3},{20,4},{21,5},{22,6},{23,7},{24,8},{25... | collective-permute-start | bytes 196616 | tf_op jit(solution)/shard_map/ppermute | solution.py:125
  66.7 38.4 %all-to-all-start = ((f32[256,2,128]{2,1,0:T(2,128)}), f32[256,2,128]{2,1,0:T(2,128)S(1)}, u32[]{:S(2)}, u32[]{:S(2)}) async-start(f32[256,2,128]{2,1,0:T(2,128)} %broadcast_in_dim.254), calls=%async_computation | async-start | bytes 524288 | tf_op jit(solution)/shard_map/all_to_all | solution.py:53
  89.9 6.4 %collective-permute-start.11 = (f32[4,8,512]{2,1,0:T(8,128)S(1)}, f32[4,8,512]{2,1,0:T(8,128)S(1)}, u32[]{:S(2)}, u32[]{:S(2)}) collective-permute-start(f32[4,8,512]{2,1,0:T(8,128)S(1)} %copy.102), channel_id=1, source_target_pairs={{0,16},{1,17},{2,18},{3,19},{4,20},{5,21},{6,22},{7,23},{8,24},{9,... | collective-permute-start | bytes 196616 | tf_op jit(solution)/shard_map/ppermute | solution.py:125
  107.5 22.1 %all-to-all-start.1 = ((f32[256,2,128]{2,1,0:T(2,128)}), f32[256,2,128]{2,1,0:T(2,128)S(1)}, u32[]{:S(2)}, u32[]{:S(2)}) async-start(f32[256,2,128]{2,1,0:T(2,128)} %broadcast_in_dim.256), calls=%async_computation.1 | async-start | bytes 524288 | tf_op jit(solution)/shard_map/all_to_all | solution.py:53
  151.6 27.7 %all-to-all-start.3 = ((f32[16,112,128]{2,1,0:T(8,128)}), f32[16,112,128]{2,1,0:T(8,128)S(1)}, u32[]{:S(2)}, u32[]{:S(2)}) async-start(f32[16,112,128]{2,1,0:T(8,128)} %broadcast_in_dim.261), calls=%async_computation.3 | async-start | bytes 1835008 | tf_op jit(solution)/shard_map/all_to_all | solution.py:53
  155.3 14.4 %collective-permute-start.17 = (f32[32,256]{1,0:T(8,128)S(1)}, f32[32,256]{1,0:T(8,128)S(1)}, u32[]{:S(2)}, u32[]{:S(2)}) collective-permute-start(f32[32,256]{1,0:T(8,128)S(1)} %get-tuple-element.39), channel_id=1, source_target_pairs={{0,16},{1,17},{2,18},{3,19},{4,20},{5,21},{6,22},{7,23},{8,24},{9,... | collective-permute-start | bytes 98312 | tf_op jit(solution)/shard_map/ppermute | solution.py:97
  160.0 11.7 %collective-permute-start.16 = (f32[32,256]{1,0:T(8,128)S(1)}, f32[32,256]{1,0:T(8,128)S(1)}, u32[]{:S(2)}, u32[]{:S(2)}) collective-permute-start(f32[32,256]{1,0:T(8,128)S(1)} %get-tuple-element.38), channel_id=1, source_target_pairs={{16,0},{17,1},{18,2},{19,3},{20,4},{21,5},{22,6},{23,7},{24,8},{25... | collective-permute-start | bytes 98312 | tf_op jit(solution)/shard_map/ppermute | solution.py:97
  161.3 10.4 %collective-permute-start.15 = (f32[32,256]{1,0:T(8,128)S(1)}, f32[32,256]{1,0:T(8,128)S(1)}, u32[]{:S(2)}, u32[]{:S(2)}) collective-permute-start(f32[32,256]{1,0:T(8,128)S(1)} %get-tuple-element.37), channel_id=1, source_target_pairs={{0,4},{1,5},{2,6},{3,7},{4,8},{5,9},{6,10},{7,11},{8,12},{9,13},{1... | collective-permute-start | bytes 98312 | tf_op jit(solution)/shard_map/ppermute | solution.py:97
  164.3 7.5 %collective-permute-start.14 = (f32[32,256]{1,0:T(8,128)S(1)}, f32[32,256]{1,0:T(8,128)S(1)}, u32[]{:S(2)}, u32[]{:S(2)}) collective-permute-start(f32[32,256]{1,0:T(8,128)S(1)} %get-tuple-element.36), channel_id=1, source_target_pairs={{4,0},{5,1},{6,2},{7,3},{8,4},{9,5},{10,6},{11,7},{12,8},{13,9},{1... | collective-permute-start | bytes 98312 | tf_op jit(solution)/shard_map/ppermute | solution.py:97
  165.6 6.2 %collective-permute-start.13 = (f32[32,256]{1,0:T(8,128)S(1)}, f32[32,256]{1,0:T(8,128)S(1)}, u32[]{:S(2)}, u32[]{:S(2)}) collective-permute-start(f32[32,256]{1,0:T(8,128)S(1)} %get-tuple-element.35), channel_id=1, source_target_pairs={{0,1},{1,2},{2,3},{4,5},{5,6},{6,7},{8,9},{9,10},{10,11},{12,13},{... | collective-permute-start | bytes 98312 | tf_op jit(solution)/shard_map/ppermute | solution.py:97
  169.7 5.5 %collective-permute-start.12 = (f32[32,256]{1,0:T(8,128)S(1)}, f32[32,256]{1,0:T(8,128)S(1)}, u32[]{:S(2)}, u32[]{:S(2)}) collective-permute-start(f32[32,256]{1,0:T(8,128)S(1)} %get-tuple-element.34), channel_id=1, source_target_pairs={{1,0},{2,1},{3,2},{5,4},{6,5},{7,6},{9,8},{10,9},{11,10},{13,12},{... | collective-permute-start | bytes 98312 | tf_op jit(solution)/shard_map/ppermute | solution.py:97
  191.0 14.3 %all-to-all-start.4 = ((f32[16,10,128]{2,1,0:T(8,128)}), f32[16,10,128]{2,1,0:T(8,128)S(1)}, u32[]{:S(2)}, u32[]{:S(2)}) async-start(f32[16,10,128]{2,1,0:T(8,128)} %broadcast_in_dim.270), calls=%async_computation.4 | async-start | bytes 262144 | tf_op jit(solution)/shard_map/all_to_all | solution.py:53
  206.1 21.9 %all-to-all-start.5 = ((f32[16,40,128]{2,1,0:T(8,128)}), f32[16,40,128]{2,1,0:T(8,128)S(1)}, u32[]{:S(2)}, u32[]{:S(2)}) async-start(f32[16,40,128]{2,1,0:T(8,128)} %broadcast_in_dim.273), calls=%async_computation.5 | async-start | bytes 655360 | tf_op jit(solution)/shard_map/all_to_all | solution.py:53
  239.6 12.3 %all-to-all-start.6 = ((f32[16,22,128]{2,1,0:T(8,128)}), f32[16,22,128]{2,1,0:T(8,128)S(1)}, u32[]{:S(2)}, u32[]{:S(2)}) async-start(f32[16,22,128]{2,1,0:T(8,128)} %broadcast_in_dim.275), calls=%async_computation.6 | async-start | bytes 393216 | tf_op jit(solution)/shard_map/all_to_all | solution.py:53
  253.1 26.9 %all-to-all-start.7 = ((f32[16,104,128]{2,1,0:T(8,128)}), f32[16,104,128]{2,1,0:T(8,128)S(1)}, u32[]{:S(2)}, u32[]{:S(2)}) async-start(f32[16,104,128]{2,1,0:T(8,128)} %broadcast_in_dim.278), calls=%async_computation.7 | async-start | bytes 1703936 | tf_op jit(solution)/shard_map/all_to_all | solution.py:53
  256.8 14.9 %collective-permute-start.23 = (f32[32,256]{1,0:T(8,128)S(1)}, f32[32,256]{1,0:T(8,128)S(1)}, u32[]{:S(2)}, u32[]{:S(2)}) collective-permute-start(f32[32,256]{1,0:T(8,128)S(1)} %get-tuple-element.33), channel_id=1, source_target_pairs={{0,16},{1,17},{2,18},{3,19},{4,20},{5,21},{6,22},{7,23},{8,24},{9,... | collective-permute-start | bytes 98312 | tf_op jit(solution)/shard_map/ppermute | solution.py:97
  262.5 11.2 %collective-permute-start.22 = (f32[32,256]{1,0:T(8,128)S(1)}, f32[32,256]{1,0:T(8,128)S(1)}, u32[]{:S(2)}, u32[]{:S(2)}) collective-permute-start(f32[32,256]{1,0:T(8,128)S(1)} %get-tuple-element.32), channel_id=1, source_target_pairs={{16,0},{17,1},{18,2},{19,3},{20,4},{21,5},{22,6},{23,7},{24,8},{25... | collective-permute-start | bytes 98312 | tf_op jit(solution)/shard_map/ppermute | solution.py:97
  263.8 9.9 %collective-permute-start.21 = (f32[32,256]{1,0:T(8,128)S(1)}, f32[32,256]{1,0:T(8,128)S(1)}, u32[]{:S(2)}, u32[]{:S(2)}) collective-permute-start(f32[32,256]{1,0:T(8,128)S(1)} %get-tuple-element.31), channel_id=1, source_target_pairs={{0,4},{1,5},{2,6},{3,7},{4,8},{5,9},{6,10},{7,11},{8,12},{9,13},{1... | collective-permute-start | bytes 98312 | tf_op jit(solution)/shard_map/ppermute | solution.py:97
  266.7 7.1 %collective-permute-start.20 = (f32[32,256]{1,0:T(8,128)S(1)}, f32[32,256]{1,0:T(8,128)S(1)}, u32[]{:S(2)}, u32[]{:S(2)}) collective-permute-start(f32[32,256]{1,0:T(8,128)S(1)} %get-tuple-element.30), channel_id=1, source_target_pairs={{4,0},{5,1},{6,2},{7,3},{8,4},{9,5},{10,6},{11,7},{12,8},{13,9},{1... | collective-permute-start | bytes 98312 | tf_op jit(solution)/shard_map/ppermute | solution.py:97
  268.0 5.8 %collective-permute-start.19 = (f32[32,256]{1,0:T(8,128)S(1)}, f32[32,256]{1,0:T(8,128)S(1)}, u32[]{:S(2)}, u32[]{:S(2)}) collective-permute-start(f32[32,256]{1,0:T(8,128)S(1)} %get-tuple-element.29), channel_id=1, source_target_pairs={{0,1},{1,2},{2,3},{4,5},{5,6},{6,7},{8,9},{9,10},{10,11},{12,13},{... | collective-permute-start | bytes 98312 | tf_op jit(solution)/shard_map/ppermute | solution.py:97
  271.7 5.5 %collective-permute-start.18 = (f32[32,256]{1,0:T(8,128)S(1)}, f32[32,256]{1,0:T(8,128)S(1)}, u32[]{:S(2)}, u32[]{:S(2)}) collective-permute-start(f32[32,256]{1,0:T(8,128)S(1)} %get-tuple-element.28), channel_id=1, source_target_pairs={{1,0},{2,1},{3,2},{5,4},{6,5},{7,6},{9,8},{10,9},{11,10},{13,12},{... | collective-permute-start | bytes 98312 | tf_op jit(solution)/shard_map/ppermute | solution.py:97
  (2 other events, 7.4 us)

commit v2 on v0

v2 whole, which is shorter than its diff:
```python
import functools

import jax
import jax.numpy as jnp
from jax import lax
from jax.experimental import pallas as pl
from jax.experimental.pallas import tpu as pltpu
from jax.sharding import PartitionSpec as P

BLK = 128
NM = 6
PM = 8
CASES = 32
ROWS = 1536
WIN = 2 * BLK
WIDE = ROWS + WIN
GX = 16
GY = 4
GZ = 4
PLANE = GY * GZ
N = GX * PLANE
SLOTS = 8 * PM
PIECES = 6
LIMIT = 48
STEPS = ((0, 0, 1), (0, 0, -1), (0, 1, 0), (0, -1, 0), (1, 0, 0), (-1, 0, 0))
STRIDES = tuple(a * PLANE + b * GZ + c for a, b, c in STEPS)
HIGHEST = lax.Precision.HIGHEST
SMEM = pl.BlockSpec(memory_space=pltpu.SMEM)
VMEM = pl.BlockSpec(memory_space=pltpu.VMEM)


def route(step):
    pairs = []
    for s in range(N):
        place = (s // PLANE, s // GZ % GY, s % GZ)
        moved = [p + d for p, d in zip(place, step)]
        if all(0 <= m < size for m, size in zip(moved, (GX, GY, GZ))):
            pairs.append((s, (moved[0] * GY + moved[1]) * GZ + moved[2]))
    return pairs


ROUTES = [route(step) for step in STEPS]
IN_PLANE = [[a * PLANE + b for b in range(PLANE)] for a in range(GX)]
ACROSS = [[a * PLANE + b for a in range(GX)] for b in range(PLANE)]


def bar(values):
    return lax.optimization_barrier(values)


def swap(block, groups):
    return lax.all_to_all(block, "dom", 0, 0, tiled=True, axis_index_groups=groups)


def trade(parts, dirs):
    return {d ^ 1: lax.ppermute(p, "dom", ROUTES[d]) for p, d in zip(parts, dirs)}


def shaped(*shape):
    return jax.ShapeDtypeStruct(shape, jnp.float32)


def dot(a, b):
    return jnp.dot(a, b, precision=HIGHEST, preferred_element_type=jnp.float32)


def dot_t(a, b):
    return lax.dot_general(
        a, b, (((1,), (1,)), ((), ())), precision=HIGHEST, preferred_element_type=jnp.float32
    )


def split(x):
    high = x.astype(jnp.bfloat16)
    rest = x - high.astype(jnp.float32)
    middle = rest.astype(jnp.bfloat16)
    return high, middle, (rest - middle.astype(jnp.float32)).astype(jnp.bfloat16)


def products(stack, m, b, contract=0):
    high, middle, low = split(b)

    def product(x, y):
        return lax.dot_general(
            x, y, (((1,), (contract,)), ((), ())), preferred_element_type=jnp.float32
        )

    first, second = product(stack, high), product(stack[: 2 * m], middle)
    small = first[2 * m :] + second[m:] + product(stack[:m], low)
    return first[:m] + (first[m : 2 * m] + second[:m] + small)


def dot6(a, b, contract=0):
    return products(jnp.concatenate(split(a), axis=0), a.shape[0], b, contract)


def move(tile, source, target):
    by = (target - source) % 128
    return tile if by == 0 else pltpu.roll(tile, by, 1)


def lanes_between(lane, low, size):
    return (lane >= low) & (lane < low + size)


def edges(table):
    out = []
    for stride in STRIDES:
        start, size = jnp.int32(0), jnp.int32(0)
        for e in range(6):
            hit = (table[0, e] == table[4, 1] + stride) & (table[2, e] > 0)
            start = jnp.where(hit, table[1, e], start)
            size = jnp.where(hit, table[2, e], size)
        out.append((pl.multiple_of(start * BLK, BLK), size * BLK))
    return out


def line_place(table):
    return lax.shift_right_logical(table[4, 1], 4)


def plane_place(table):
    return lax.bitwise_and(table[4, 1], PLANE - 1)


def put_near(table, field_ref, near_ref, first_row):
    rows = field_ref.shape[0]
    near_ref[:, first_row:, :] = jnp.zeros((PLANE, 2 * rows, 128), jnp.float32)
    for d, (start, size) in list(enumerate(edges(table)))[:4]:

        @pl.when(size > 0)
        def _():
            to = plane_place(table) + STRIDES[d]
            window = field_ref[:, pl.ds(start, WIN)]
            near_ref[to, first_row : first_row + rows, :] = window[:, :BLK]
            near_ref[to, first_row + rows : first_row + 2 * rows, :] = window[:, BLK:]


def get_faces(table, near_ref, first_row, rows, up_ref, down_ref):
    lane = lax.broadcasted_iota(jnp.int32, (rows, WIN), 1)
    out = []
    for d, (start, size) in enumerate(edges(table)):
        if d < 4:
            at = jnp.clip(plane_place(table) + STRIDES[d], 0, PLANE - 1)
            face = jnp.concatenate(
                [
                    near_ref[at, first_row : first_row + rows, :],
                    near_ref[at, first_row + rows : first_row + 2 * rows, :],
                ],
                axis=1,
            )
        else:
            face = (up_ref if d == 4 else down_ref)[...]
        out.append((start, jnp.where(lane < size, face, 0.0)))
    return out


def setup_kernel(
    table, modes_ref, coarse_ref, gaps_ref, field_ref, sign_ref, parcel_ref, near_ref, up_ref, down_ref, pad_ref
):
    block = lax.shift_right_logical(lax.broadcasted_iota(jnp.int32, (1, ROWS), 1), 7)
    sign = jnp.zeros((1, ROWS), jnp.int32)
    for e in range(6):
        inside = (block >= table[1, e]) & (block < table[1, e] + table[2, e])
        sign = sign + jnp.where(inside, table[3, e], 0)
    sign = sign.astype(jnp.float32)
    sign_ref[...] = sign
    field_ref[:, ROWS:] = jnp.zeros((CASES + PM, WIN), jnp.float32)
    field_ref[:CASES, :ROWS] = gaps_ref[...] * sign
    mode = lax.broadcasted_iota(jnp.int32, (NM, ROWS), 0)
    field_ref[CASES:, :ROWS] = jnp.zeros((PM, ROWS), jnp.float32)
    field_ref[CASES : CASES + NM, :ROWS] = jnp.where(mode < table[4, 0], modes_ref[...] * sign, 0.0)
    pad_ref[...] = jnp.zeros((PM, WIDE), jnp.float32)
    pad_ref[:NM, :ROWS] = coarse_ref[...]
    padded = pad_ref[...]
    planes = [padded[:, :128]]
    for i in range(1, GX):
        planes.append(pltpu.roll(padded, (WIDE - PLANE * NM * i) % WIDE, 1)[:, :128])
    row, col = (lax.broadcasted_iota(jnp.int32, (128, 128), a) for a in (0, 1))
    part = lax.bitwise_and(col, PM - 1)
    source = lax.shift_right_logical(col, 3) * NM + part
    widen = jnp.where((row == source) & (part < NM), 1.0, 0.0)
    wide = dot(jnp.concatenate(planes, axis=0), widen)
    zero = jnp.zeros((PM, 128), jnp.float32)
    for i in range(GX):
        for t in range(3):
            p = i + t - 1
            parcel_ref[i, :, 128 * t : 128 * (t + 1)] = (
                wide[PM * p : PM * (p + 1)] if 0 <= p < GX else zero
            )
    put_near(table, field_ref, near_ref, 0)
    where = edges(table)
    up_ref[...] = field_ref[:, pl.ds(where[4][0], WIN)]
    down_ref[...] = field_ref[:, pl.ds(where[5][0], WIN)]


def start_kernel(
    table, field_ref, near_ref, up_ref, down_ref, parcel_ref, rhs_ref, lifts_ref, weights_ref, message_ref, gram_ref, sum_ref, wide_ref
):
    sum_ref[...] = field_ref[:CASES, :]
    wide_ref[...] = jnp.zeros((SLOTS, WIDE), jnp.float32)
    wide_ref[:PM, :] = field_ref[CASES:, :]
    for d, (start, face) in enumerate(get_faces(table, near_ref, 0, CASES + PM, up_ref, down_ref)):
        sum_ref[:, pl.ds(start, WIN)] += face[:CASES]
        wide_ref[PM * (d + 1) : PM * (d + 2), pl.ds(start, WIN)] = face[CASES:]
    rhs = sum_ref[:, :ROWS]
    lifts = wide_ref[:, :ROWS]
    rhs_ref[...] = rhs
    lifts_ref[...] = lifts
    modes = lifts[:PM]
    weights = dot6(modes, rhs, 1)
    weights_ref[...] = weights
    message_ref[:, :PM, :] = jnp.zeros((GX, PM, 128), jnp.float32)
    message_ref[:, :PM, :CASES] = jnp.broadcast_to(weights[None], (GX, PM, CASES))
    for t in range(3):
        message_ref[:, PM * (t + 1) : PM * (t + 2), :] = parcel_ref[:, :, 128 * t : 128 * (t + 1)]
    gram_ref[...] = dot6(modes, lifts, 1)


def summed(second_ref, rows):
    total = second_ref[0, :rows]
    for q in range(1, PLANE):
        total = total + second_ref[q, :rows]
    return total


def pack(tile):
    half = CASES // 2
    return tile[:half] + pltpu.roll(tile[half:], 64, 1)


def unpack(total):
    return jnp.concatenate([total, pltpu.roll(total, 64, 1)], axis=0)


def next_kernel(from_slot, second_ref, weights_ref, gram_ref, total_ref, message_ref):
    total = summed(second_ref, CASES) if from_slot else unpack(summed(second_ref, CASES // 2))
    total_ref[...] = total
    own = total[:, 7 * PM : 8 * PM].T if from_slot else weights_ref[...]
    weights = own - dot6(gram_ref[:, : 7 * PM], total[:, : 7 * PM], 1)
    message_ref[...] = jnp.zeros((GX, PM, 128), jnp.float32)
    message_ref[:, :, :CASES] = jnp.broadcast_to(weights[None], (GX, PM, CASES))


def spread(coeffs, lane, extra, put):
    below, here, above = (coeffs[:, 128 * t : 128 * (t + 1)] for t in range(3))
    for q in range(PLANE):
        tile = extra(q)
        pieces = [(here, q, 0), (here, q - 1, 2), (here, q + 4, 3), (here, q - 4, 4), (above, q, 5), (below, q, 6)]
        for plane, source, slot in pieces:
            moved = move(plane, source * PM, slot * PM)
            size = 2 * PM if slot == 0 else PM
            tile = jnp.where(lanes_between(lane, slot * PM, size), moved, tile)
        put(q, tile)


def combine(weights, coarse, out_ref):
    lane = lax.broadcasted_iota(jnp.int32, (CASES, 128), 1)
    coeffs = dot6(weights.reshape(GX * PM, 128).T[:CASES], coarse)
    zero = jnp.zeros((CASES, 128), jnp.float32)

    def put(q, tile):
        out_ref[q] = pack(tile)

    spread(coeffs, lane, lambda q: zero, put)


def combine_kernel(first_ref, coarse_ref, out_ref):
    combine(first_ref[...], coarse_ref[...], out_ref)


def combine_first_kernel(first_ref, out_ref, coarse_ref, block_ref):
    for t in range(3):
        part = first_ref[:, PM * (t + 1) : PM * (t + 2), :].reshape(GX * PM, 128)
        coarse_ref[:, 128 * t : 128 * (t + 1)] = part
    for i in range(GX):
        block_ref[NM * i : NM * (i + 1), :] = coarse_ref[PM * i : PM * i + NM, :]
    combine(first_ref[:, :PM, :], coarse_ref[...], out_ref)


def combine_terms_kernel(with_slot, table, first_ref, image_ref, *refs):
    coarse_refs, (out_ref, up_ref, down_ref) = refs[:5], refs[5:]
    lane = lax.broadcasted_iota(jnp.int32, (CASES, 128), 1)
    zero = jnp.zeros((CASES, 128), jnp.float32)
    tiles = [first_ref[i] for i in range(GX)]
    total = tiles[0]
    for tile in tiles[1:]:
        total = total + tile

    def collect(slot, by, size=PM):
        out = zero
        for i in range(GX):
            if 0 <= i + by < GX:
                moved = move(tiles[i + by], slot * PM, i * size)
                out = jnp.where(lanes_between(lane, i * size, size), moved, out)
        return out

    line = collect(0, 0) + collect(5, -1) + collect(6, 1)
    coeffs = dot6(line, coarse_refs[0][...])
    for d in range(4):
        coeffs = coeffs + dot6(collect(d + 1, 0, NM)[:, : GX * NM], coarse_refs[d + 1][...])
    if with_slot:
        sums = jnp.where(lane >= 8 * PM, total, 0.0)
        mine = first_ref[line_place(table)]
        base = 7 * PM
        from_line = pltpu.roll(line, lax.rem(base - line_place(table) * PM + 128, 128), 1)
        slots = [(0, from_line)] + [(STRIDES[d], move(mine, (d + 1) * PM, base)) for d in range(4)]
        in_slot = lanes_between(lane, base, PM)

        def extra(q):
            tile = sums
            for by, value in slots:
                tile = jnp.where(in_slot & (plane_place(table) + by == q), value, tile)
            return tile

    else:
        sums = jnp.where(lane >= 7 * PM, total, 0.0)

        def extra(q):
            return sums

    def put(q, tile):
        out_ref[q, :CASES] = tile

    spread(coeffs, lane, extra, put)
    put_near(table, image_ref, out_ref, CASES)
    where = edges(table)
    up_ref[...] = image_ref[:, pl.ds(where[4][0], WIN)]
    down_ref[...] = image_ref[:, pl.ds(where[5][0], WIN)]


def fetch(schur_ref, block_ref, sems):
    size = ROWS // PIECES
    copies = []
    for p in range(PIECES):
        rows = pl.ds(p * size, size)
        copies.append(pltpu.make_async_copy(schur_ref.at[rows], block_ref.at[rows], sems.at[p]))
        copies[-1].start()
    return copies


def schur_product(field, sign, copies, stack_ref, block_ref):
    size = ROWS // PIECES
    m = field.shape[0]
    stack_ref[...] = jnp.concatenate(split(field * sign), axis=0)
    total = jnp.zeros((m, ROWS), jnp.float32)
    for p in range(PIECES):
        copies[p].wait()
        rows = slice(p * size, (p + 1) * size)
        total = total + products(stack_ref[:, rows], m, block_ref[rows, :])
    return total * sign


def schur_first_kernel(rhs_ref, lifts_ref, sign_ref, schur_ref, rhs_out_ref, lifts_out_ref, sign_out_ref, stack_ref, block_ref, sems):
    copies = fetch(schur_ref, block_ref, sems)
    field = jnp.concatenate([rhs_ref[...], lifts_ref[...]], axis=0)
    out = schur_product(field, sign_ref[...], copies, stack_ref, block_ref)
    rhs_out_ref[...] = out[:CASES]
    lifts_out_ref[...] = out[CASES:]
    sign_out_ref[...] = sign_ref[...]


def base_kernel(total_ref, rhs_ref, lifts_ref, start_ref, gram_ref):
    start = rhs_ref[...] - dot6(total_ref[:, : 7 * PM], lifts_ref[: 7 * PM, :])
    start_ref[...] = start
    gram_ref[...] = dot6(start, start, 1)


def terms_first_kernel(
    second_ref, before_ref, rhs_ref, rhs_schur_ref, lifts_ref, lifts_schur_ref, gram_ref, image_ref, message_ref, coeffs_ref
):
    coeffs = unpack(summed(second_ref, CASES // 2))
    coeffs_ref[...] = coeffs
    whole = (before_ref[...] + coeffs)[:, : 7 * PM]
    field = rhs_ref[...] - dot6(whole, lifts_ref[: 7 * PM, :])
    image = rhs_schur_ref[...] - dot6(whole, lifts_schur_ref[: 7 * PM, :])
    image_ref[:, :ROWS] = image
    image_ref[:, ROWS:] = jnp.zeros((CASES, WIN), jnp.float32)
    tile = [dot6(image, lifts_ref[...], 1), 2.0 * dot6(field, image, 1), gram_ref[...]]
    message_ref[...] = jnp.broadcast_to(jnp.concatenate(tile, axis=1)[None], (GX, CASES, 128))


def terms_last_kernel(
    third_ref, before_ref, step_ref, residual_ref, lifts_ref, sign_ref, old_image_ref, schur_ref,
    image_ref, message_ref, stack_ref, block_ref, sems
):
    copies = fetch(schur_ref, block_ref, sems)
    coeffs = before_ref[...] - dot(step_ref[...].T, unpack(summed(third_ref, CASES // 2)))
    residual = residual_ref[...]
    field = residual - dot6(coeffs[:, : 7 * PM], lifts_ref[: 7 * PM, :])
    gram = dot6(residual, residual, 1)
    cross = 2.0 * dot6(field, old_image_ref[:, :ROWS], 1)
    image = schur_product(field, sign_ref[...], copies, stack_ref, block_ref)
    image_ref[:, :ROWS] = image
    image_ref[:, ROWS:] = jnp.zeros((CASES, WIN), jnp.float32)
    curvature = 2.0 * dot6(field, image, 1)
    row, col = (lax.broadcasted_iota(jnp.int32, (CASES, CASES), a) for a in (0, 1))
    diagonal = jnp.sum(jnp.where(row == col, gram, 0.0), axis=1, keepdims=True)
    lane = lax.broadcasted_iota(jnp.int32, (CASES, SLOTS), 1)
    terms = jnp.where(lane == 7 * PM, diagonal, dot6(image, lifts_ref[...], 1))
    tile = jnp.concatenate([terms, jnp.where(row >= col, curvature, gram), cross], axis=1)
    message_ref[...] = jnp.broadcast_to(tile[None], (GX, CASES, 128))


def solve(matrix, target):
    row_id = lax.broadcasted_iota(jnp.int32, target.shape, 0)
    columns = [jnp.broadcast_to(matrix[:, j : j + 1], target.shape) for j in range(CASES)]
    for k in range(CASES):
        column = columns[k]
        inverse = 1.0 / column[k : k + 1, :]
        pivot = row_id == k

        def eliminate(x):
            row = x[k : k + 1, :] * inverse
            return jnp.where(pivot, row, x - column * row)

        for j in range(k + 1, CASES):
            columns[j] = eliminate(columns[j])
        target = eliminate(target)
    return target


def assembled(table, image_ref, second_ref, up_ref, down_ref, sum_ref):
    sum_ref[...] = image_ref[...]
    for start, face in get_faces(table, second_ref, CASES, CASES, up_ref, down_ref):
        sum_ref[:, pl.ds(start, WIN)] += face
    return sum_ref[:, :ROWS]


def middle_kernel(
    table, total_ref, image_ref, second_ref, up_ref, down_ref, lifts_ref, start_ref, step_ref, inverse_ref, image_out_ref, residual_ref, sum_ref
):
    total = total_ref[...]
    full = assembled(table, image_ref, second_ref, up_ref, down_ref, sum_ref)
    full = full - dot6(total[:, : 7 * PM], lifts_ref[: 7 * PM, :])
    image_out_ref[...] = full
    row, col = (lax.broadcasted_iota(jnp.int32, (CASES, CASES), a) for a in (0, 1))
    steplen = solve(total[:, 64:96], total[:, 96:])
    step_ref[...] = steplen
    inverse_ref[...] = solve(total[:, 96:], jnp.where(row == col, 1.0, 0.0))
    residual_ref[...] = start_ref[...] - dot6(steplen.T, full)


def last_kernel(
    table, image_ref, second_ref, up_ref, down_ref, lifts_ref, start_ref, residual_ref, old_image_ref, step_ref, inverse_ref, sums_ref,
    solution_out_ref, residual_out_ref, sum_ref
):
    total = summed(second_ref, CASES)
    row, col = (lax.broadcasted_iota(jnp.int32, (CASES, CASES), a) for a in (0, 1))
    mixed = total[:, 64:96]
    flipped = mixed.T
    gram = jnp.where(row < col, mixed, jnp.where(row > col, flipped, total[:, 7 * PM : 7 * PM + 1]))
    curvature = jnp.where(row >= col, mixed, flipped)
    beta = dot(inverse_ref[...], gram)
    crossed = dot(total[:, 96:], beta)
    curvature = curvature + crossed + crossed.T + dot(beta.T, dot(sums_ref[:, 64:96], beta))
    steplen = solve(curvature, gram)
    old_step = dot(beta, steplen)
    full = assembled(table, image_ref, second_ref, up_ref, down_ref, sum_ref)
    full = full - dot6(total[:, : 7 * PM], lifts_ref[: 7 * PM, :])
    residual = residual_ref[...]
    solution_out_ref[...] = dot6((step_ref[...] + old_step).T, start_ref[...]) + dot6(steplen.T, residual)
    residual_out_ref[...] = residual - dot6(steplen.T, full) - dot6(old_step.T, old_image_ref[...])


def call(kernel, outs, *args, smem=0, scratch=()):
    return pl.pallas_call(
        kernel,
        out_shape=outs,
        in_specs=[SMEM] * smem + [VMEM] * (len(args) - smem),
        out_specs=jax.tree.map(lambda _: VMEM, outs),
        scratch_shapes=[pltpu.VMEM(s, jnp.float32) for s in scratch],
        compiler_params=pltpu.CompilerParams(vmem_limit_bytes=32 * 2**20),
    )(*args)


def schur_call(kernel, outs, rows, *args):
    return pl.pallas_call(
        kernel,
        out_shape=outs,
        in_specs=[VMEM] * (len(args) - 1) + [pl.BlockSpec(memory_space=pltpu.HBM)],
        out_specs=jax.tree.map(lambda _: VMEM, outs),
        scratch_shapes=[
            pltpu.VMEM((3 * rows, ROWS), jnp.bfloat16),
            pltpu.VMEM((ROWS, ROWS), jnp.float32),
            pltpu.SemaphoreType.DMA((PIECES,)),
        ],
        cost_estimate=pl.CostEstimate(
            flops=12 * rows * ROWS * ROWS, bytes_accessed=4 * ROWS * ROWS, transcendentals=0
        ),
        compiler_params=pltpu.CompilerParams(vmem_limit_bytes=48 * 2**20),
    )(*args)


def shards(
    schur_blocks,
    rigid_modes,
    coarse_inverse,
    local_gaps,
    glue_peer,
    glue_offset,
    glue_count,
    glue_sign,
    mode_counts,
):
    me = lax.axis_index("dom").astype(jnp.int32)
    last_row = jnp.stack([mode_counts[0], me, me, me, me, me])[None]
    table = jnp.concatenate([glue_peer, glue_offset, glue_count, glue_sign, last_row], axis=0)

    field, sign, parcel, near, up, down = call(
        setup_kernel,
        [
            shaped(CASES + PM, WIDE),
            shaped(1, ROWS),
            shaped(GX, PM, 384),
            shaped(PLANE, 2 * (CASES + PM), 128),
            shaped(CASES + PM, WIN),
            shaped(CASES + PM, WIN),
        ],
        table,
        rigid_modes,
        coarse_inverse,
        local_gaps,
        smem=1,
        scratch=[(PM, WIDE)],
    )
    near = swap(near, IN_PLANE)
    got = trade([up, down], (4, 5))
    dual_rhs, lifts, weights, message, own_gram = call(
        start_kernel,
        [
            shaped(CASES, ROWS),
            shaped(SLOTS, ROWS),
            shaped(PM, CASES),
            shaped(GX, CASES, 128),
            shaped(PM, SLOTS),
        ],
        table,
        field,
        near,
        got[4],
        got[5],
        parcel,
        smem=1,
        scratch=[(CASES, WIDE), (SLOTS, WIDE)],
    )
    packed = shaped(PLANE, CASES // 2, 128)
    whole_field = shaped(CASES, ROWS)
    square = shaped(CASES, CASES)
    rhs_schur, lifts_schur, sign = schur_call(
        schur_first_kernel,
        [whole_field, shaped(SLOTS, ROWS), shaped(1, ROWS)],
        CASES + SLOTS,
        dual_rhs,
        lifts,
        sign,
        schur_blocks,
    )
    terms_outs = [shaped(CASES, WIDE), shaped(GX, CASES, 128)]

    def sync_terms(with_slot, message, image):
        first = swap(message, ACROSS)
        tiles, up, down = call(
            functools.partial(combine_terms_kernel, with_slot),
            [shaped(PLANE, 3 * CASES, 128), shaped(CASES, WIN), shaped(CASES, WIN)],
            table,
            first,
            image,
            own_coarse,
            *[blocks[d] for d in range(4)],
            smem=1,
        )
        second = swap(tiles, IN_PLANE)
        got = trade([up, down], (4, 5))
        if with_slot:
            return bar((second, got[4], got[5]))
        return second, got[4], got[5]

    def next_weights(from_slot, second, weights):
        return call(
            functools.partial(next_kernel, from_slot),
            [shaped(CASES, 128), shaped(GX, PM, 128)],
            second,
            weights,
            own_gram,
        )

    first, sign = bar((swap(message, ACROSS), sign))
    tiles, own_coarse, block = call(
        combine_first_kernel, [packed, shaped(GX * PM, 384), shaped(GX * NM, 384)], first
    )
    second = swap(tiles, IN_PLANE)
    total, message = next_weights(False, second, weights)
    first = swap(message, ACROSS)
    tiles = call(combine_kernel, packed, first, own_coarse)
    tiles, block = bar((tiles, block))
    second = swap(tiles, IN_PLANE)
    blocks = trade([block] * 4, range(4))
    start, start_gram = call(base_kernel, [whole_field, square], total, dual_rhs, lifts)

    image, message, start_coeffs = call(
        terms_first_kernel,
        terms_outs + [shaped(CASES, 128)],
        second,
        total,
        dual_rhs,
        rhs_schur,
        lifts,
        lifts_schur,
        start_gram,
    )
    second, up, down = sync_terms(True, message, image)
    total, message = next_weights(True, second, weights)
    first = swap(message, ACROSS)
    third = swap(call(combine_kernel, packed, first, own_coarse), IN_PLANE)
    steplen, inverse, proj_image, residual = call(
        middle_kernel,
        [square, square, whole_field, whole_field],
        table,
        total,
        image,
        second,
        up,
        down,
        lifts,
        start,
        smem=1,
        scratch=[(CASES, WIDE)],
    )

    image, message = schur_call(
        terms_last_kernel,
        terms_outs,
        CASES,
        third,
        start_coeffs,
        steplen,
        residual,
        lifts,
        sign,
        image,
        schur_blocks,
    )
    second, up, down = sync_terms(False, message, image)
    return tuple(
        call(
            last_kernel,
            [shaped(CASES, ROWS), shaped(CASES, ROWS)],
            table,
            image,
            second,
            up,
            down,
            lifts,
            start,
            residual,
            proj_image,
            steplen,
            inverse,
            total,
            smem=1,
            scratch=[(CASES, WIDE)],
        )
    )


def solution(mesh):
    return jax.shard_map(
        shards,
        mesh=mesh,
        in_specs=(
            P("dom", None),
            P("dom", None),
            P("dom", None),
            P(None, "dom"),
            P("dom", None),
            P("dom", None),
            P("dom", None),
            P("dom", None),
            P("dom"),
        ),
        out_specs=(P(None, "dom"), P(None, "dom")),
        check_vma=False,
    )
```

time: 1790 us -> 209 us (0.12)
  waiting for transfers between devices: 1260 us -> 39.5 us
  blocking collectives: 255 us -> 58.4 us
  starting transfers between devices: 191 us -> 73.2 us
  matrix products: 35.2 us -> 0 us
  Pallas kernels: 0 us -> 31.8 us
  other arithmetic: 24.2 us -> 0 us
  between operations: 23.3 us -> 1.45 us
    psum x5 -> x0, waiting for transfers between devices: 1240 us -> none  [coarse_coeffs(): whole = lax.psum(term, 'dom')]
    psum x3 -> x0, blocking collectives: 255 us -> none  [the longest x1 87.1 us: shards(): res_gram = lax.psum(inner_product(residual, residual), 'dom')]
    ppermute x48 -> x10, starting transfers between devices: 191 us -> 30.2 us  [trade(): lax.ppermute(p, 'dom', ROUTES[d])]
    all_to_all x0 -> x4, blocking collectives: none -> 58.4 us  [swap(): lax.all_to_all(block, 'dom', 0, 0, tiled=True, axis_index_groups=groups)]
    all_to_all x0 -> x7, starting transfers between devices: none -> 43 us  [swap(): lax.all_to_all(block, 'dom', 0, 0, tiled=True, axis_index_groups=groups)]
    dot_general x26 -> x0, matrix products: 34.2 us -> none  [the longest x2 15.8 us: shards(): jnp.dot(row_sign * projected, schur_blocks, precision=highest, preferred_...]
    pallas_call x0 -> x15, Pallas kernels: none -> 31.8 us  [the longest x13 21.1 us: call(): pl.pallas_call(kernel, out_shape=outs, in_specs=[SMEM] * smem + [VMEM] *...]
    another operation x15 -> x0, other arithmetic: 20 us -> none  [the longest x9 10.8 us: gram_solve(): jnp.linalg.cholesky(matrix)]
  transfers between devices with their start and end apart: 53 -> 17, of which waited for: 20 -> 12; matrix products, arithmetic and copies ran while one was open for 0% -> 0% of each run, Pallas kernels for 0% -> 4%
where the time goes in v2:
time: 209 us; the launch traced here: 208 us
  starting transfers between devices  73.2 us (35%)
  blocking collectives  58.4 us (28%)
  waiting for transfers between devices  39.5 us (19%)
  Pallas kernels  31.8 us (15%)
  local copies, waits for them, and re-layouts  3.33 us (2%)
    all_to_all x4, blocking collectives, swap(): lax.all_to_all(block, 'dom', 0, 0, tiled=True, axis_index_groups=groups)  58.4 us
    all_to_all x7, starting transfers between devices, swap(): lax.all_to_all(block, 'dom', 0, 0, tiled=True, axis_index_groups=groups)  43 us
    ppermute x10, starting transfers between devices, trade(): lax.ppermute(p, 'dom', ROUTES[d])  30.2 us
    pallas_call x13, Pallas kernels, call(): pl.pallas_call(kernel, out_shape=outs, in_specs=[SMEM] * smem + [VMEM] *...  21.1 us
    ppermute x10, waiting for transfers between devices, trade(): lax.ppermute(p, 'dom', ROUTES[d])  20.2 us
    all_to_all x7, waiting for transfers between devices, swap(): lax.all_to_all(block, 'dom', 0, 0, tiled=True, axis_index_groups=groups)  19.2 us
    pallas_call x2, Pallas kernels, schur_call(): pl.pallas_call(kernel, out_shape=outs, in_specs=[VMEM] * (len(args) - 1)...  10.7 us
  transfers between devices with their start and end apart: 17, of which 12 were waited for; matrix products, arithmetic and copies ran while one was open for 0% of the time, Pallas kernels for 4%

profile of v2, /device:TPU:1, one launch (start us, length us, event | category | flops | bytes accessed | tf_op | source)
XLA Modules:
  0.0 207.6 jit_solution(11816310678416112694)
XLA Ops:
  6.4 6.9 %all-to-all-start = ((f32[16,80,128]{2,1,0:T(8,128)}), f32[16,80,128]{2,1,0:T(8,128)S(1)}, u32[]{:S(2)}, u32[]{:S(2)}) async-start(f32[16,80,128]{2,1,0:T(8,128)} %get-tuple-element.48), calls=%async_computation | async-start | bytes 1310720 | tf_op jit(solution)/shard_map/all_to_all | solution.py:52
  14.6 5.5 %collective-permute-start.1 = (f32[40,256]{1,0:T(8,128)S(1)}, f32[40,256]{1,0:T(8,128)S(1)}, u32[]{:S(2)}, u32[]{:S(2)}) collective-permute-start(f32[40,256]{1,0:T(8,128)S(1)} %get-tuple-element.50), channel_id=1, source_target_pairs={{0,16},{1,17},{2,18},{3,19},{4,20},{5,21},{6,22},{7,23},{8,24},{9,... | collective-permute-start | bytes 122888 | tf_op jit(solution)/shard_map/ppermute | solution.py:56
  20.2 4.9 %collective-permute-done.up_ref = f32[40,256]{1,0:T(8,128)S(1)} collective-permute-done((f32[40,256]{1,0:T(8,128)S(1)}, f32[40,256]{1,0:T(8,128)S(1)}, u32[]{:S(2)}, u32[]{:S(2)}) %collective-permute-start) | collective-permute-done | bytes 40992 | tf_op jit(solution)/shard_map/ppermute | solution.py:56
  27.2 9.6 %all-to-all-start.1 = ((f32[16,32,128]{2,1,0:T(8,128)}), f32[16,32,128]{2,1,0:T(8,128)S(1)}, u32[]{:S(2)}, u32[]{:S(2)}) async-start(f32[16,32,128]{2,1,0:T(8,128)} %get-tuple-element.52), calls=%async_computation.1 | async-start | bytes 524288 | tf_op jit(solution)/shard_map/all_to_all | solution.py:52
  36.7 4.9 %shard_map.106 = (f32[32,1536]{1,0:T(8,128)S(1)}, f32[64,1536]{1,0:T(8,128)S(1)}, f32[1,1536]{1,0:T(1,128)S(1)}) custom-call(f32[32,1536]{1,0:T(8,128)S(1)} %get-tuple-element.53.rhs_ref, f32[64,1536]{1,0:T(8,128)S(1)} %get-tuple-element.54.lifts_ref, f32[1,1536]{1,0:T(1,128)S(1)} %get-tuple-element.55.sign_ref, f32[1536,1536]{1,0:T(8,128)} %schur_ref.3), custom_call_target="tpu_custom_call" | custom-call | flops 2717908992 | bytes 9437184 | tf_op jit(solution)/shard_map/pallas_call | solution.py:478
  41.7 6.3 %all-to-all-done.1.first_ref = f32[16,32,128]{2,1,0:T(8,128)S(1)} async-done(((f32[16,32,128]{2,1,0:T(8,128)}), f32[16,32,128]{2,1,0:T(8,128)S(1)}, u32[]{:S(2)}, u32[]{:S(2)}) %all-to-all-start.1) | async-done | bytes 262176 | tf_op jit(solution)/shard_map/all_to_all | solution.py:52
  48.6 13.4 %all_to_all.55.second_ref = f32[16,16,128]{2,1,0:T(8,128)S(1)} all-to-all(f32[16,16,128]{2,1,0:T(8,128)S(1)} %get-tuple-element.58), channel_id=1, replica_groups={{0,1,2,3,4,5,6,7,8,9,10,11,12,13,14,15},{16,17,18,19,20,21,22,23,24,25,..., dimensions={0} | all-to-all | bytes 262144 | tf_op jit(solution)/shard_map/all_to_all | solution.py:52
  62.2 12.0 %all_to_all.56.first_ref = f32[16,8,128]{2,1,0:T(8,128)S(1)} all-to-all(f32[16,8,128]{2,1,0:T(8,128)S(1)} %get-tuple-element.61), channel_id=1, replica_groups={{0,16,32,48,64,80,96,112,128,144,160,176,192,208,224,240},{1,17,33,49,6..., dimensions={0} | all-to-all | bytes 131072 | tf_op jit(solution)/shard_map/all_to_all | solution.py:52
  75.5 5.4 %all-to-all-start.4 = ((f32[16,16,128]{2,1,0:T(8,128)}), f32[16,16,128]{2,1,0:T(8,128)S(1)}, u32[]{:S(2)}, u32[]{:S(2)}) async-start(f32[16,16,128]{2,1,0:T(8,128)} %shard_map.109), calls=%async_computation.4 | async-start | bytes 262144 | tf_op jit(solution)/shard_map/all_to_all | solution.py:52
  81.6 5.5 %all-to-all-done.4.second_ref = f32[16,16,128]{2,1,0:T(8,128)S(1)} async-done(((f32[16,16,128]{2,1,0:T(8,128)}), f32[16,16,128]{2,1,0:T(8,128)S(1)}, u32[]{:S(2)}, u32[]{:S(2)}) %all-to-all-start.4) | async-done | bytes 131104 | tf_op jit(solution)/shard_map/all_to_all | solution.py:52
  88.9 3.5 %all-to-all-start.5 = ((f32[16,32,128]{2,1,0:T(8,128)}), f32[16,32,128]{2,1,0:T(8,128)S(1)}, u32[]{:S(2)}, u32[]{:S(2)}) async-start(f32[16,32,128]{2,1,0:T(8,128)} %get-tuple-element.69), calls=%async_computation.5 | async-start | bytes 524288 | tf_op jit(solution)/shard_map/all_to_all | solution.py:52
  92.4 2.8 %collective-permute-start.5 = (f32[96,384]{1,0:T(8,128)S(1)}, f32[96,384]{1,0:T(8,128)S(1)}, u32[]{:S(2)}, u32[]{:S(2)}) collective-permute-start(f32[96,384]{1,0:T(8,128)S(1)} %get-tuple-element.71), channel_id=1, source_target_pairs={{0,4},{1,5},{2,6},{3,7},{4,8},{5,9},{6,10},{7,11},{8,12},{9,13},{1... | collective-permute-start | bytes 442376 | tf_op jit(solution)/shard_map/ppermute | solution.py:56
  96.5 3.1 %collective-permute-start.3 = (f32[96,384]{1,0:T(8,128)S(1)}, f32[96,384]{1,0:T(8,128)S(1)}, u32[]{:S(2)}, u32[]{:S(2)}) collective-permute-start(f32[96,384]{1,0:T(8,128)S(1)} %get-tuple-element.71), channel_id=1, source_target_pairs={{0,1},{1,2},{2,3},{4,5},{5,6},{6,7},{8,9},{9,10},{10,11},{12,13},{... | collective-permute-start | bytes 442376 | tf_op jit(solution)/shard_map/ppermute | solution.py:56
  99.7 1.9 collective-permute-start.2
  101.6 1.9 collective-permute-done.4.refs_3_
  104.9 2.0 collective-permute-done.2.refs_1_
  106.9 2.5 %shard_map.112 = (f32[16,96,128]{2,1,0:T(8,128)}, f32[32,256]{1,0:T(8,128)S(1)}, f32[32,256]{1,0:T(8,128)S(1)}) custom-call(s32[5,6]{1,0:T(8,128)S(1)} %concatenate.3.table, f32[16,32,128]{2,1,0:T(8,128)S(1)} %all-to-all-done.5.first_ref, f32[32,1792]{1,0:T(8,128)S(1)} %get-tuple-element.70.image_ref.old_image_ref, ...), custom_call_target="tpu_custom_call" | custom-call | tf_op jit(solution)/shard_map/pallas_call | solution.py:467
  109.4 5.4 %all-to-all-start.6 = ((f32[16,96,128]{2,1,0:T(8,128)}), f32[16,96,128]{2,1,0:T(8,128)S(1)}, u32[]{:S(2)}, u32[]{:S(2)}) async-start(f32[16,96,128]{2,1,0:T(8,128)} %get-tuple-element.72), calls=%async_computation.6 | async-start | bytes 1572864 | tf_op jit(solution)/shard_map/all_to_all | solution.py:52
  116.1 6.1 %collective-permute-start.7 = (f32[32,256]{1,0:T(8,128)S(1)}, f32[32,256]{1,0:T(8,128)S(1)}, u32[]{:S(2)}, u32[]{:S(2)}) collective-permute-start(f32[32,256]{1,0:T(8,128)S(1)} %get-tuple-element.74), channel_id=1, source_target_pairs={{0,16},{1,17},{2,18},{3,19},{4,20},{5,21},{6,22},{7,23},{8,24},{9,... | collective-permute-start | bytes 98312 | tf_op jit(solution)/shard_map/ppermute | solution.py:56
  122.2 6.6 %collective-permute-done.6.up_ref = f32[32,256]{1,0:T(8,128)S(1)} collective-permute-done((f32[32,256]{1,0:T(8,128)S(1)}, f32[32,256]{1,0:T(8,128)S(1)}, u32[]{:S(2)}, u32[]{:S(2)}) %collective-permute-start.6) | collective-permute-done | bytes 32800 | tf_op jit(solution)/shard_map/ppermute | solution.py:56
  129.0 18.1 %all_to_all.57.first_ref = f32[16,8,128]{2,1,0:T(8,128)S(1)} all-to-all(f32[16,8,128]{2,1,0:T(8,128)S(1)} %get-tuple-element.76), channel_id=1, replica_groups={{0,16,32,48,64,80,96,112,128,144,160,176,192,208,224,240},{1,17,33,49,6..., dimensions={0} | all-to-all | bytes 131072 | tf_op jit(solution)/shard_map/all_to_all | solution.py:52
  148.3 6.2 %all-to-all-start.8 = ((f32[16,16,128]{2,1,0:T(8,128)}), f32[16,16,128]{2,1,0:T(8,128)S(1)}, u32[]{:S(2)}, u32[]{:S(2)}) async-start(f32[16,16,128]{2,1,0:T(8,128)} %shard_map.114), calls=%async_computation.8 | async-start | bytes 262144 | tf_op jit(solution)/shard_map/all_to_all | solution.py:52
  154.6 2.7 %shard_map.115 = (f32[32,32]{1,0:T(8,128)S(1)}, f32[32,32]{1,0:T(8,128)S(1)}, f32[32,1536]{1,0:T(8,128)S(1)}, f32[32,1536]{1,0:T(8,128)S(1)}) custom-call(s32[5,6]{1,0:T(8,128)S(1)} %concatenate.3.table, f32[32,128]{1,0:T(8,128)S(1)} %get-tuple-element.78.total_ref.sums_ref, f32[32,1792]{1,0:T(8,128)S(1)} %get-tuple-element.70.image_ref.old_image_ref, ...), custom_call_target="tpu_custom_call" | custom-call | tf_op jit(solution)/shard_map/pallas_call | solution.py:467
  157.2 3.5 %all-to-all-done.8.third_ref = f32[16,16,128]{2,1,0:T(8,128)S(1)} async-done(((f32[16,16,128]{2,1,0:T(8,128)}), f32[16,16,128]{2,1,0:T(8,128)S(1)}, u32[]{:S(2)}, u32[]{:S(2)}) %all-to-all-start.8) | async-done | bytes 131104 | tf_op jit(solution)/shard_map/all_to_all | solution.py:52
  160.8 5.7 %shard_map.116 = (f32[32,1792]{1,0:T(8,128)S(1)}, f32[16,32,128]{2,1,0:T(8,128)S(1)}) custom-call(f32[16,16,128]{2,1,0:T(8,128)S(1)} %all-to-all-done.8.third_ref, f32[32,128]{1,0:T(8,128)S(1)} %get-tuple-element.77.before_ref, f32[32,32]{1,0:T(8,128)S(1)} %get-tuple-element.82.step_ref, f32[32,1536]{1,0:T(8,128)S(1)} %get-tuple-element.83.residual_ref, ...), custom_call_target="tpu_custom_call" | custom-call | flops 905969664 | bytes 9437184 | tf_op jit(solution)/shard_map/pallas_call | solution.py:478
  166.5 15.0 %all_to_all.58.first_ref = f32[16,32,128]{2,1,0:T(8,128)S(1)} all-to-all(f32[16,32,128]{2,1,0:T(8,128)S(1)} %get-tuple-element.86), channel_id=1, replica_groups={{0,16,32,48,64,80,96,112,128,144,160,176,192,208,224,240},{1,17,33,49,6..., dimensions={0} | all-to-all | bytes 524288 | tf_op jit(solution)/shard_map/all_to_all | solution.py:52
  181.5 2.5 %shard_map.117 = (f32[16,96,128]{2,1,0:T(8,128)}, f32[32,256]{1,0:T(8,128)S(1)}, f32[32,256]{1,0:T(8,128)S(1)}) custom-call(s32[5,6]{1,0:T(8,128)S(1)} %concatenate.3.table, f32[16,32,128]{2,1,0:T(8,128)S(1)} %all_to_all.58.first_ref, f32[32,1792]{1,0:T(8,128)S(1)} %get-tuple-element.85.image_ref, f32[128,384]{1,0:T(8,128)S(1)} %get-tuple-element.62.coarse_ref.refs_0_, ...), custom_call_target="tpu_custom_call" | custom-call | tf_op jit(solution)/shard_map/pallas_call | solution.py:467
  184.0 5.9 %all-to-all-start.10 = ((f32[16,96,128]{2,1,0:T(8,128)}), f32[16,96,128]{2,1,0:T(8,128)S(1)}, u32[]{:S(2)}, u32[]{:S(2)}) async-start(f32[16,96,128]{2,1,0:T(8,128)} %get-tuple-element.87), calls=%async_computation.10 | async-start | bytes 1572864 | tf_op jit(solution)/shard_map/all_to_all | solution.py:52
  191.3 5.5 %collective-permute-start.9 = (f32[32,256]{1,0:T(8,128)S(1)}, f32[32,256]{1,0:T(8,128)S(1)}, u32[]{:S(2)}, u32[]{:S(2)}) collective-permute-start(f32[32,256]{1,0:T(8,128)S(1)} %get-tuple-element.89), channel_id=1, source_target_pairs={{0,16},{1,17},{2,18},{3,19},{4,20},{5,21},{6,22},{7,23},{8,24},{9,... | collective-permute-start | bytes 98312 | tf_op jit(solution)/shard_map/ppermute | solution.py:56
  196.8 3.3 %collective-permute-done.8.up_ref = f32[32,256]{1,0:T(8,128)S(1)} collective-permute-done((f32[32,256]{1,0:T(8,128)S(1)}, f32[32,256]{1,0:T(8,128)S(1)}, u32[]{:S(2)}, u32[]{:S(2)}) %collective-permute-start.8) | collective-permute-done | bytes 32800 | tf_op jit(solution)/shard_map/ppermute | solution.py:56
  200.2 3.5 %all-to-all-done.10.second_ref = f32[16,96,128]{2,1,0:T(8,128)S(1)} async-done(((f32[16,96,128]{2,1,0:T(8,128)}), f32[16,96,128]{2,1,0:T(8,128)S(1)}, u32[]{:S(2)}, u32[]{:S(2)}) %all-to-all-start.10) | async-done | bytes 786464 | tf_op jit(solution)/shard_map/all_to_all | solution.py:52
  203.7 3.9 %shard_map.118 = (f32[32,1536]{1,0:T(8,128)}, f32[32,1536]{1,0:T(8,128)}) custom-call(s32[5,6]{1,0:T(8,128)S(1)} %concatenate.3.table, f32[32,1792]{1,0:T(8,128)S(1)} %get-tuple-element.85.image_ref, f32[16,96,128]{2,1,0:T(8,128)S(1)} %all-to-all-done.10.second_ref, f32[32,256]{1,0:T(8,128)S(1)} %collective-permute-done.8.up_ref, ...), custom_call_target="tpu_custom_call" | custom-call | tf_op jit(solution)/shard_map/pallas_call | solution.py:467
  (29 shorter events, 20.0 us)
Async XLA Ops:
  2.1 0.9 copy-start
  3.0 0.8 copy-start.1
  3.8 0.8 copy-start.2
  6.4 19.0 %all-to-all-start = ((f32[16,80,128]{2,1,0:T(8,128)}), f32[16,80,128]{2,1,0:T(8,128)S(1)}, u32[]{:S(2)}, u32[]{:S(2)}) async-start(f32[16,80,128]{2,1,0:T(8,128)} %get-tuple-element.48), calls=%async_computation | async-start | bytes 1310720 | tf_op jit(solution)/shard_map/all_to_all | solution.py:52
  13.4 11.7 %collective-permute-start = (f32[40,256]{1,0:T(8,128)S(1)}, f32[40,256]{1,0:T(8,128)S(1)}, u32[]{:S(2)}, u32[]{:S(2)}) collective-permute-start(f32[40,256]{1,0:T(8,128)S(1)} %get-tuple-element.49), channel_id=1, source_target_pairs={{16,0},{17,1},{18,2},{19,3},{20,4},{21,5},{22,6},{23,7},{24,8},{25... | collective-permute-start | bytes 122888 | tf_op jit(solution)/shard_map/ppermute | solution.py:56
  14.6 10.4 %collective-permute-start.1 = (f32[40,256]{1,0:T(8,128)S(1)}, f32[40,256]{1,0:T(8,128)S(1)}, u32[]{:S(2)}, u32[]{:S(2)}) collective-permute-start(f32[40,256]{1,0:T(8,128)S(1)} %get-tuple-element.50), channel_id=1, source_target_pairs={{0,16},{1,17},{2,18},{3,19},{4,20},{5,21},{6,22},{7,23},{8,24},{9,... | collective-permute-start | bytes 122888 | tf_op jit(solution)/shard_map/ppermute | solution.py:56
  27.2 20.8 %all-to-all-start.1 = ((f32[16,32,128]{2,1,0:T(8,128)}), f32[16,32,128]{2,1,0:T(8,128)S(1)}, u32[]{:S(2)}, u32[]{:S(2)}) async-start(f32[16,32,128]{2,1,0:T(8,128)} %get-tuple-element.52), calls=%async_computation.1 | async-start | bytes 524288 | tf_op jit(solution)/shard_map/all_to_all | solution.py:52
  75.5 11.6 %all-to-all-start.4 = ((f32[16,16,128]{2,1,0:T(8,128)}), f32[16,16,128]{2,1,0:T(8,128)S(1)}, u32[]{:S(2)}, u32[]{:S(2)}) async-start(f32[16,16,128]{2,1,0:T(8,128)} %shard_map.109), calls=%async_computation.4 | async-start | bytes 262144 | tf_op jit(solution)/shard_map/all_to_all | solution.py:52
  88.9 18.0 %all-to-all-start.5 = ((f32[16,32,128]{2,1,0:T(8,128)}), f32[16,32,128]{2,1,0:T(8,128)S(1)}, u32[]{:S(2)}, u32[]{:S(2)}) async-start(f32[16,32,128]{2,1,0:T(8,128)} %get-tuple-element.69), calls=%async_computation.5 | async-start | bytes 524288 | tf_op jit(solution)/shard_map/all_to_all | solution.py:52
  92.4 9.2 %collective-permute-start.5 = (f32[96,384]{1,0:T(8,128)S(1)}, f32[96,384]{1,0:T(8,128)S(1)}, u32[]{:S(2)}, u32[]{:S(2)}) collective-permute-start(f32[96,384]{1,0:T(8,128)S(1)} %get-tuple-element.71), channel_id=1, source_target_pairs={{0,4},{1,5},{2,6},{3,7},{4,8},{5,9},{6,10},{7,11},{8,12},{9,13},{1... | collective-permute-start | bytes 442376 | tf_op jit(solution)/shard_map/ppermute | solution.py:56
  95.2 8.2 %collective-permute-start.4 = (f32[96,384]{1,0:T(8,128)S(1)}, f32[96,384]{1,0:T(8,128)S(1)}, u32[]{:S(2)}, u32[]{:S(2)}) collective-permute-start(f32[96,384]{1,0:T(8,128)S(1)} %get-tuple-element.71), channel_id=1, source_target_pairs={{4,0},{5,1},{6,2},{7,3},{8,4},{9,5},{10,6},{11,7},{12,8},{13,9},{1... | collective-permute-start | bytes 442376 | tf_op jit(solution)/shard_map/ppermute | solution.py:56
  96.5 8.4 %collective-permute-start.3 = (f32[96,384]{1,0:T(8,128)S(1)}, f32[96,384]{1,0:T(8,128)S(1)}, u32[]{:S(2)}, u32[]{:S(2)}) collective-permute-start(f32[96,384]{1,0:T(8,128)S(1)} %get-tuple-element.71), channel_id=1, source_target_pairs={{0,1},{1,2},{2,3},{4,5},{5,6},{6,7},{8,9},{9,10},{10,11},{12,13},{... | collective-permute-start | bytes 442376 | tf_op jit(solution)/shard_map/ppermute | solution.py:56
  99.7 7.2 %collective-permute-start.2 = (f32[96,384]{1,0:T(8,128)S(1)}, f32[96,384]{1,0:T(8,128)S(1)}, u32[]{:S(2)}, u32[]{:S(2)}) collective-permute-start(f32[96,384]{1,0:T(8,128)S(1)} %get-tuple-element.71), channel_id=1, source_target_pairs={{1,0},{2,1},{3,2},{5,4},{6,5},{7,6},{9,8},{10,9},{11,10},{13,12},{... | collective-permute-start | bytes 442376 | tf_op jit(solution)/shard_map/ppermute | solution.py:56
  109.4 19.5 %all-to-all-start.6 = ((f32[16,96,128]{2,1,0:T(8,128)}), f32[16,96,128]{2,1,0:T(8,128)S(1)}, u32[]{:S(2)}, u32[]{:S(2)}) async-start(f32[16,96,128]{2,1,0:T(8,128)} %get-tuple-element.72), calls=%async_computation.6 | async-start | bytes 1572864 | tf_op jit(solution)/shard_map/all_to_all | solution.py:52
  114.8 14.0 %collective-permute-start.6 = (f32[32,256]{1,0:T(8,128)S(1)}, f32[32,256]{1,0:T(8,128)S(1)}, u32[]{:S(2)}, u32[]{:S(2)}) collective-permute-start(f32[32,256]{1,0:T(8,128)S(1)} %get-tuple-element.73), channel_id=1, source_target_pairs={{16,0},{17,1},{18,2},{19,3},{20,4},{21,5},{22,6},{23,7},{24,8},{25... | collective-permute-start | bytes 98312 | tf_op jit(solution)/shard_map/ppermute | solution.py:56
  116.1 12.8 %collective-permute-start.7 = (f32[32,256]{1,0:T(8,128)S(1)}, f32[32,256]{1,0:T(8,128)S(1)}, u32[]{:S(2)}, u32[]{:S(2)}) collective-permute-start(f32[32,256]{1,0:T(8,128)S(1)} %get-tuple-element.74), channel_id=1, source_target_pairs={{0,16},{1,17},{2,18},{3,19},{4,20},{5,21},{6,22},{7,23},{8,24},{9,... | collective-permute-start | bytes 98312 | tf_op jit(solution)/shard_map/ppermute | solution.py:56
  148.3 12.4 %all-to-all-start.8 = ((f32[16,16,128]{2,1,0:T(8,128)}), f32[16,16,128]{2,1,0:T(8,128)S(1)}, u32[]{:S(2)}, u32[]{:S(2)}) async-start(f32[16,16,128]{2,1,0:T(8,128)} %shard_map.114), calls=%async_computation.8 | async-start | bytes 262144 | tf_op jit(solution)/shard_map/all_to_all | solution.py:52
  184.0 19.7 %all-to-all-start.10 = ((f32[16,96,128]{2,1,0:T(8,128)}), f32[16,96,128]{2,1,0:T(8,128)S(1)}, u32[]{:S(2)}, u32[]{:S(2)}) async-start(f32[16,96,128]{2,1,0:T(8,128)} %get-tuple-element.87), calls=%async_computation.10 | async-start | bytes 1572864 | tf_op jit(solution)/shard_map/all_to_all | solution.py:52
  190.0 10.1 %collective-permute-start.8 = (f32[32,256]{1,0:T(8,128)S(1)}, f32[32,256]{1,0:T(8,128)S(1)}, u32[]{:S(2)}, u32[]{:S(2)}) collective-permute-start(f32[32,256]{1,0:T(8,128)S(1)} %get-tuple-element.88), channel_id=1, source_target_pairs={{16,0},{17,1},{18,2},{19,3},{20,4},{21,5},{22,6},{23,7},{24,8},{25... | collective-permute-start | bytes 98312 | tf_op jit(solution)/shard_map/ppermute | solution.py:56
  191.3 9.0 %collective-permute-start.9 = (f32[32,256]{1,0:T(8,128)S(1)}, f32[32,256]{1,0:T(8,128)S(1)}, u32[]{:S(2)}, u32[]{:S(2)}) collective-permute-start(f32[32,256]{1,0:T(8,128)S(1)} %get-tuple-element.89), channel_id=1, source_target_pairs={{0,16},{1,17},{2,18},{3,19},{4,20},{5,21},{6,22},{7,23},{8,24},{9,... | collective-permute-start | bytes 98312 | tf_op jit(solution)/shard_map/ppermute | solution.py:56

commit v3 on v2

--- a/solution.py
+++ b/solution.py
@@ -459,8 +459,11 @@
     full = assembled(table, image_ref, second_ref, up_ref, down_ref, sum_ref)
     full = full - dot6(total[:, : 7 * PM], lifts_ref[: 7 * PM, :])
     residual = residual_ref[...]
-    solution_out_ref[...] = dot6((step_ref[...] + old_step).T, start_ref[...]) + dot6(steplen.T, residual)
-    residual_out_ref[...] = residual - dot6(steplen.T, full) - dot6(old_step.T, old_image_ref[...])
+    steps = jnp.concatenate([step_ref[...] + old_step, steplen], axis=0)
+    solution_out_ref[...] = dot6(steps.T, jnp.concatenate([start_ref[...], residual], axis=0))
+    steps = jnp.concatenate([steplen, old_step], axis=0)
+    fields = jnp.concatenate([full, old_image_ref[...]], axis=0)
+    residual_out_ref[...] = residual - dot6(steps.T, fields)
 
 
 def call(kernel, outs, *args, smem=0, scratch=()):

time: 209 us -> 209 us (level)
  no operation moved by 1% of the time
where the time goes in v3:
time: 209 us; the launch traced here: 207 us
  starting transfers between devices  73.2 us (35%)
  blocking collectives  58.4 us (28%)
  waiting for transfers between devices  39.5 us (19%)
  Pallas kernels  31.5 us (15%)
  local copies, waits for them, and re-layouts  3.33 us (2%)
    all_to_all x4, blocking collectives, swap(): lax.all_to_all(block, 'dom', 0, 0, tiled=True, axis_index_groups=groups)  58.4 us
    all_to_all x7, starting transfers between devices, swap(): lax.all_to_all(block, 'dom', 0, 0, tiled=True, axis_index_groups=groups)  43 us
    ppermute x10, starting transfers between devices, trade(): lax.ppermute(p, 'dom', ROUTES[d])  30.2 us
    pallas_call x13, Pallas kernels, call(): pl.pallas_call(kernel, out_shape=outs, in_specs=[SMEM] * smem + [VMEM] *...  20.8 us
    ppermute x10, waiting for transfers between devices, trade(): lax.ppermute(p, 'dom', ROUTES[d])  20.2 us
    all_to_all x7, waiting for transfers between devices, swap(): lax.all_to_all(block, 'dom', 0, 0, tiled=True, axis_index_groups=groups)  19.2 us
    pallas_call x2, Pallas kernels, schur_call(): pl.pallas_call(kernel, out_shape=outs, in_specs=[VMEM] * (len(args) - 1)...  10.7 us
  transfers between devices with their start and end apart: 17, of which 12 were waited for; matrix products, arithmetic and copies ran while one was open for 0% of the time, Pallas kernels for 4%

profile of v3, /device:TPU:1, one launch (start us, length us, event | category | flops | bytes accessed | tf_op | source)
XLA Modules:
  0.0 207.3 jit_solution(7584697967200267045)
XLA Ops:
  6.4 6.9 %all-to-all-start = ((f32[16,80,128]{2,1,0:T(8,128)}), f32[16,80,128]{2,1,0:T(8,128)S(1)}, u32[]{:S(2)}, u32[]{:S(2)}) async-start(f32[16,80,128]{2,1,0:T(8,128)} %get-tuple-element.48), calls=%async_computation | async-start | bytes 1310720 | tf_op jit(solution)/shard_map/all_to_all | solution.py:52
  14.6 5.5 %collective-permute-start.1 = (f32[40,256]{1,0:T(8,128)S(1)}, f32[40,256]{1,0:T(8,128)S(1)}, u32[]{:S(2)}, u32[]{:S(2)}) collective-permute-start(f32[40,256]{1,0:T(8,128)S(1)} %get-tuple-element.50), channel_id=1, source_target_pairs={{0,16},{1,17},{2,18},{3,19},{4,20},{5,21},{6,22},{7,23},{8,24},{9,... | collective-permute-start | bytes 122888 | tf_op jit(solution)/shard_map/ppermute | solution.py:56
  20.2 4.9 %collective-permute-done.up_ref = f32[40,256]{1,0:T(8,128)S(1)} collective-permute-done((f32[40,256]{1,0:T(8,128)S(1)}, f32[40,256]{1,0:T(8,128)S(1)}, u32[]{:S(2)}, u32[]{:S(2)}) %collective-permute-start) | collective-permute-done | bytes 40992 | tf_op jit(solution)/shard_map/ppermute | solution.py:56
  27.2 9.6 %all-to-all-start.1 = ((f32[16,32,128]{2,1,0:T(8,128)}), f32[16,32,128]{2,1,0:T(8,128)S(1)}, u32[]{:S(2)}, u32[]{:S(2)}) async-start(f32[16,32,128]{2,1,0:T(8,128)} %get-tuple-element.52), calls=%async_computation.1 | async-start | bytes 524288 | tf_op jit(solution)/shard_map/all_to_all | solution.py:52
  36.7 4.9 %shard_map.106 = (f32[32,1536]{1,0:T(8,128)S(1)}, f32[64,1536]{1,0:T(8,128)S(1)}, f32[1,1536]{1,0:T(1,128)S(1)}) custom-call(f32[32,1536]{1,0:T(8,128)S(1)} %get-tuple-element.53.rhs_ref, f32[64,1536]{1,0:T(8,128)S(1)} %get-tuple-element.54.lifts_ref, f32[1,1536]{1,0:T(1,128)S(1)} %get-tuple-element.55.sign_ref, f32[1536,1536]{1,0:T(8,128)} %schur_ref.3), custom_call_target="tpu_custom_call" | custom-call | flops 2717908992 | bytes 9437184 | tf_op jit(solution)/shard_map/pallas_call | solution.py:481
  41.7 6.3 %all-to-all-done.1.first_ref = f32[16,32,128]{2,1,0:T(8,128)S(1)} async-done(((f32[16,32,128]{2,1,0:T(8,128)}), f32[16,32,128]{2,1,0:T(8,128)S(1)}, u32[]{:S(2)}, u32[]{:S(2)}) %all-to-all-start.1) | async-done | bytes 262176 | tf_op jit(solution)/shard_map/all_to_all | solution.py:52
  48.6 13.4 %all_to_all.55.second_ref = f32[16,16,128]{2,1,0:T(8,128)S(1)} all-to-all(f32[16,16,128]{2,1,0:T(8,128)S(1)} %get-tuple-element.58), channel_id=1, replica_groups={{0,1,2,3,4,5,6,7,8,9,10,11,12,13,14,15},{16,17,18,19,20,21,22,23,24,25,..., dimensions={0} | all-to-all | bytes 262144 | tf_op jit(solution)/shard_map/all_to_all | solution.py:52
  62.2 12.0 %all_to_all.56.first_ref = f32[16,8,128]{2,1,0:T(8,128)S(1)} all-to-all(f32[16,8,128]{2,1,0:T(8,128)S(1)} %get-tuple-element.61), channel_id=1, replica_groups={{0,16,32,48,64,80,96,112,128,144,160,176,192,208,224,240},{1,17,33,49,6..., dimensions={0} | all-to-all | bytes 131072 | tf_op jit(solution)/shard_map/all_to_all | solution.py:52
  75.5 5.4 %all-to-all-start.4 = ((f32[16,16,128]{2,1,0:T(8,128)}), f32[16,16,128]{2,1,0:T(8,128)S(1)}, u32[]{:S(2)}, u32[]{:S(2)}) async-start(f32[16,16,128]{2,1,0:T(8,128)} %shard_map.109), calls=%async_computation.4 | async-start | bytes 262144 | tf_op jit(solution)/shard_map/all_to_all | solution.py:52
  81.6 5.5 %all-to-all-done.4.second_ref = f32[16,16,128]{2,1,0:T(8,128)S(1)} async-done(((f32[16,16,128]{2,1,0:T(8,128)}), f32[16,16,128]{2,1,0:T(8,128)S(1)}, u32[]{:S(2)}, u32[]{:S(2)}) %all-to-all-start.4) | async-done | bytes 131104 | tf_op jit(solution)/shard_map/all_to_all | solution.py:52
  88.9 3.5 %all-to-all-start.5 = ((f32[16,32,128]{2,1,0:T(8,128)}), f32[16,32,128]{2,1,0:T(8,128)S(1)}, u32[]{:S(2)}, u32[]{:S(2)}) async-start(f32[16,32,128]{2,1,0:T(8,128)} %get-tuple-element.69), calls=%async_computation.5 | async-start | bytes 524288 | tf_op jit(solution)/shard_map/all_to_all | solution.py:52
  92.4 2.8 %collective-permute-start.5 = (f32[96,384]{1,0:T(8,128)S(1)}, f32[96,384]{1,0:T(8,128)S(1)}, u32[]{:S(2)}, u32[]{:S(2)}) collective-permute-start(f32[96,384]{1,0:T(8,128)S(1)} %get-tuple-element.71), channel_id=1, source_target_pairs={{0,4},{1,5},{2,6},{3,7},{4,8},{5,9},{6,10},{7,11},{8,12},{9,13},{1... | collective-permute-start | bytes 442376 | tf_op jit(solution)/shard_map/ppermute | solution.py:56
  96.5 3.1 %collective-permute-start.3 = (f32[96,384]{1,0:T(8,128)S(1)}, f32[96,384]{1,0:T(8,128)S(1)}, u32[]{:S(2)}, u32[]{:S(2)}) collective-permute-start(f32[96,384]{1,0:T(8,128)S(1)} %get-tuple-element.71), channel_id=1, source_target_pairs={{0,1},{1,2},{2,3},{4,5},{5,6},{6,7},{8,9},{9,10},{10,11},{12,13},{... | collective-permute-start | bytes 442376 | tf_op jit(solution)/shard_map/ppermute | solution.py:56
  99.7 1.9 collective-permute-start.2
  101.6 1.9 collective-permute-done.4.refs_3_
  104.9 1.9 collective-permute-done.2.refs_1_
  106.9 2.5 %shard_map.112 = (f32[16,96,128]{2,1,0:T(8,128)}, f32[32,256]{1,0:T(8,128)S(1)}, f32[32,256]{1,0:T(8,128)S(1)}) custom-call(s32[5,6]{1,0:T(8,128)S(1)} %concatenate.3.table, f32[16,32,128]{2,1,0:T(8,128)S(1)} %all-to-all-done.5.first_ref, f32[32,1792]{1,0:T(8,128)S(1)} %get-tuple-element.70.image_ref.old_image_ref, ...), custom_call_target="tpu_custom_call" | custom-call | tf_op jit(solution)/shard_map/pallas_call | solution.py:470
  109.4 5.4 %all-to-all-start.6 = ((f32[16,96,128]{2,1,0:T(8,128)}), f32[16,96,128]{2,1,0:T(8,128)S(1)}, u32[]{:S(2)}, u32[]{:S(2)}) async-start(f32[16,96,128]{2,1,0:T(8,128)} %get-tuple-element.72), calls=%async_computation.6 | async-start | bytes 1572864 | tf_op jit(solution)/shard_map/all_to_all | solution.py:52
  116.1 6.1 %collective-permute-start.7 = (f32[32,256]{1,0:T(8,128)S(1)}, f32[32,256]{1,0:T(8,128)S(1)}, u32[]{:S(2)}, u32[]{:S(2)}) collective-permute-start(f32[32,256]{1,0:T(8,128)S(1)} %get-tuple-element.74), channel_id=1, source_target_pairs={{0,16},{1,17},{2,18},{3,19},{4,20},{5,21},{6,22},{7,23},{8,24},{9,... | collective-permute-start | bytes 98312 | tf_op jit(solution)/shard_map/ppermute | solution.py:56
  122.3 6.6 %collective-permute-done.6.up_ref = f32[32,256]{1,0:T(8,128)S(1)} collective-permute-done((f32[32,256]{1,0:T(8,128)S(1)}, f32[32,256]{1,0:T(8,128)S(1)}, u32[]{:S(2)}, u32[]{:S(2)}) %collective-permute-start.6) | collective-permute-done | bytes 32800 | tf_op jit(solution)/shard_map/ppermute | solution.py:56
  129.0 18.1 %all_to_all.57.first_ref = f32[16,8,128]{2,1,0:T(8,128)S(1)} all-to-all(f32[16,8,128]{2,1,0:T(8,128)S(1)} %get-tuple-element.76), channel_id=1, replica_groups={{0,16,32,48,64,80,96,112,128,144,160,176,192,208,224,240},{1,17,33,49,6..., dimensions={0} | all-to-all | bytes 131072 | tf_op jit(solution)/shard_map/all_to_all | solution.py:52
  148.3 6.2 %all-to-all-start.8 = ((f32[16,16,128]{2,1,0:T(8,128)}), f32[16,16,128]{2,1,0:T(8,128)S(1)}, u32[]{:S(2)}, u32[]{:S(2)}) async-start(f32[16,16,128]{2,1,0:T(8,128)} %shard_map.114), calls=%async_computation.8 | async-start | bytes 262144 | tf_op jit(solution)/shard_map/all_to_all | solution.py:52
  154.6 2.7 %shard_map.115 = (f32[32,32]{1,0:T(8,128)S(1)}, f32[32,32]{1,0:T(8,128)S(1)}, f32[32,1536]{1,0:T(8,128)S(1)}, f32[32,1536]{1,0:T(8,128)S(1)}) custom-call(s32[5,6]{1,0:T(8,128)S(1)} %concatenate.3.table, f32[32,128]{1,0:T(8,128)S(1)} %get-tuple-element.78.total_ref.sums_ref, f32[32,1792]{1,0:T(8,128)S(1)} %get-tuple-element.70.image_ref.old_image_ref, ...), custom_call_target="tpu_custom_call" | custom-call | tf_op jit(solution)/shard_map/pallas_call | solution.py:470
  157.2 3.6 %all-to-all-done.8.third_ref = f32[16,16,128]{2,1,0:T(8,128)S(1)} async-done(((f32[16,16,128]{2,1,0:T(8,128)}), f32[16,16,128]{2,1,0:T(8,128)S(1)}, u32[]{:S(2)}, u32[]{:S(2)}) %all-to-all-start.8) | async-done | bytes 131104 | tf_op jit(solution)/shard_map/all_to_all | solution.py:52
  160.8 5.7 %shard_map.116 = (f32[32,1792]{1,0:T(8,128)S(1)}, f32[16,32,128]{2,1,0:T(8,128)S(1)}) custom-call(f32[16,16,128]{2,1,0:T(8,128)S(1)} %all-to-all-done.8.third_ref, f32[32,128]{1,0:T(8,128)S(1)} %get-tuple-element.77.before_ref, f32[32,32]{1,0:T(8,128)S(1)} %get-tuple-element.82.step_ref, f32[32,1536]{1,0:T(8,128)S(1)} %get-tuple-element.83.residual_ref, ...), custom_call_target="tpu_custom_call" | custom-call | flops 905969664 | bytes 9437184 | tf_op jit(solution)/shard_map/pallas_call | solution.py:481
  166.5 15.0 %all_to_all.58.first_ref = f32[16,32,128]{2,1,0:T(8,128)S(1)} all-to-all(f32[16,32,128]{2,1,0:T(8,128)S(1)} %get-tuple-element.86), channel_id=1, replica_groups={{0,16,32,48,64,80,96,112,128,144,160,176,192,208,224,240},{1,17,33,49,6..., dimensions={0} | all-to-all | bytes 524288 | tf_op jit(solution)/shard_map/all_to_all | solution.py:52
  181.5 2.5 %shard_map.117 = (f32[16,96,128]{2,1,0:T(8,128)}, f32[32,256]{1,0:T(8,128)S(1)}, f32[32,256]{1,0:T(8,128)S(1)}) custom-call(s32[5,6]{1,0:T(8,128)S(1)} %concatenate.3.table, f32[16,32,128]{2,1,0:T(8,128)S(1)} %all_to_all.58.first_ref, f32[32,1792]{1,0:T(8,128)S(1)} %get-tuple-element.85.image_ref, f32[128,384]{1,0:T(8,128)S(1)} %get-tuple-element.62.coarse_ref.refs_0_, ...), custom_call_target="tpu_custom_call" | custom-call | tf_op jit(solution)/shard_map/pallas_call | solution.py:470
  184.0 6.0 %all-to-all-start.10 = ((f32[16,96,128]{2,1,0:T(8,128)}), f32[16,96,128]{2,1,0:T(8,128)S(1)}, u32[]{:S(2)}, u32[]{:S(2)}) async-start(f32[16,96,128]{2,1,0:T(8,128)} %get-tuple-element.87), calls=%async_computation.10 | async-start | bytes 1572864 | tf_op jit(solution)/shard_map/all_to_all | solution.py:52
  191.3 5.5 %collective-permute-start.9 = (f32[32,256]{1,0:T(8,128)S(1)}, f32[32,256]{1,0:T(8,128)S(1)}, u32[]{:S(2)}, u32[]{:S(2)}) collective-permute-start(f32[32,256]{1,0:T(8,128)S(1)} %get-tuple-element.89), channel_id=1, source_target_pairs={{0,16},{1,17},{2,18},{3,19},{4,20},{5,21},{6,22},{7,23},{8,24},{9,... | collective-permute-start | bytes 98312 | tf_op jit(solution)/shard_map/ppermute | solution.py:56
  196.8 3.3 %collective-permute-done.8.up_ref = f32[32,256]{1,0:T(8,128)S(1)} collective-permute-done((f32[32,256]{1,0:T(8,128)S(1)}, f32[32,256]{1,0:T(8,128)S(1)}, u32[]{:S(2)}, u32[]{:S(2)}) %collective-permute-start.8) | collective-permute-done | bytes 32800 | tf_op jit(solution)/shard_map/ppermute | solution.py:56
  200.2 3.5 %all-to-all-done.10.second_ref = f32[16,96,128]{2,1,0:T(8,128)S(1)} async-done(((f32[16,96,128]{2,1,0:T(8,128)}), f32[16,96,128]{2,1,0:T(8,128)S(1)}, u32[]{:S(2)}, u32[]{:S(2)}) %all-to-all-start.10) | async-done | bytes 786464 | tf_op jit(solution)/shard_map/all_to_all | solution.py:52
  203.7 3.6 %shard_map.118 = (f32[32,1536]{1,0:T(8,128)}, f32[32,1536]{1,0:T(8,128)}) custom-call(s32[5,6]{1,0:T(8,128)S(1)} %concatenate.3.table, f32[32,1792]{1,0:T(8,128)S(1)} %get-tuple-element.85.image_ref, f32[16,96,128]{2,1,0:T(8,128)S(1)} %all-to-all-done.10.second_ref, f32[32,256]{1,0:T(8,128)S(1)} %collective-permute-done.8.up_ref, ...), custom_call_target="tpu_custom_call" | custom-call | tf_op jit(solution)/shard_map/pallas_call | solution.py:470
  (29 shorter events, 20.1 us)
Async XLA Ops:
  2.1 0.9 copy-start
  3.0 0.8 copy-start.1
  3.8 0.8 copy-start.2
  6.4 19.0 %all-to-all-start = ((f32[16,80,128]{2,1,0:T(8,128)}), f32[16,80,128]{2,1,0:T(8,128)S(1)}, u32[]{:S(2)}, u32[]{:S(2)}) async-start(f32[16,80,128]{2,1,0:T(8,128)} %get-tuple-element.48), calls=%async_computation | async-start | bytes 1310720 | tf_op jit(solution)/shard_map/all_to_all | solution.py:52
  13.4 11.7 %collective-permute-start = (f32[40,256]{1,0:T(8,128)S(1)}, f32[40,256]{1,0:T(8,128)S(1)}, u32[]{:S(2)}, u32[]{:S(2)}) collective-permute-start(f32[40,256]{1,0:T(8,128)S(1)} %get-tuple-element.49), channel_id=1, source_target_pairs={{16,0},{17,1},{18,2},{19,3},{20,4},{21,5},{22,6},{23,7},{24,8},{25... | collective-permute-start | bytes 122888 | tf_op jit(solution)/shard_map/ppermute | solution.py:56
  14.6 10.4 %collective-permute-start.1 = (f32[40,256]{1,0:T(8,128)S(1)}, f32[40,256]{1,0:T(8,128)S(1)}, u32[]{:S(2)}, u32[]{:S(2)}) collective-permute-start(f32[40,256]{1,0:T(8,128)S(1)} %get-tuple-element.50), channel_id=1, source_target_pairs={{0,16},{1,17},{2,18},{3,19},{4,20},{5,21},{6,22},{7,23},{8,24},{9,... | collective-permute-start | bytes 122888 | tf_op jit(solution)/shard_map/ppermute | solution.py:56
  27.2 20.8 %all-to-all-start.1 = ((f32[16,32,128]{2,1,0:T(8,128)}), f32[16,32,128]{2,1,0:T(8,128)S(1)}, u32[]{:S(2)}, u32[]{:S(2)}) async-start(f32[16,32,128]{2,1,0:T(8,128)} %get-tuple-element.52), calls=%async_computation.1 | async-start | bytes 524288 | tf_op jit(solution)/shard_map/all_to_all | solution.py:52
  75.5 11.6 %all-to-all-start.4 = ((f32[16,16,128]{2,1,0:T(8,128)}), f32[16,16,128]{2,1,0:T(8,128)S(1)}, u32[]{:S(2)}, u32[]{:S(2)}) async-start(f32[16,16,128]{2,1,0:T(8,128)} %shard_map.109), calls=%async_computation.4 | async-start | bytes 262144 | tf_op jit(solution)/shard_map/all_to_all | solution.py:52
  88.9 18.0 %all-to-all-start.5 = ((f32[16,32,128]{2,1,0:T(8,128)}), f32[16,32,128]{2,1,0:T(8,128)S(1)}, u32[]{:S(2)}, u32[]{:S(2)}) async-start(f32[16,32,128]{2,1,0:T(8,128)} %get-tuple-element.69), calls=%async_computation.5 | async-start | bytes 524288 | tf_op jit(solution)/shard_map/all_to_all | solution.py:52
  92.4 9.2 %collective-permute-start.5 = (f32[96,384]{1,0:T(8,128)S(1)}, f32[96,384]{1,0:T(8,128)S(1)}, u32[]{:S(2)}, u32[]{:S(2)}) collective-permute-start(f32[96,384]{1,0:T(8,128)S(1)} %get-tuple-element.71), channel_id=1, source_target_pairs={{0,4},{1,5},{2,6},{3,7},{4,8},{5,9},{6,10},{7,11},{8,12},{9,13},{1... | collective-permute-start | bytes 442376 | tf_op jit(solution)/shard_map/ppermute | solution.py:56
  95.2 8.2 %collective-permute-start.4 = (f32[96,384]{1,0:T(8,128)S(1)}, f32[96,384]{1,0:T(8,128)S(1)}, u32[]{:S(2)}, u32[]{:S(2)}) collective-permute-start(f32[96,384]{1,0:T(8,128)S(1)} %get-tuple-element.71), channel_id=1, source_target_pairs={{4,0},{5,1},{6,2},{7,3},{8,4},{9,5},{10,6},{11,7},{12,8},{13,9},{1... | collective-permute-start | bytes 442376 | tf_op jit(solution)/shard_map/ppermute | solution.py:56
  96.5 8.4 %collective-permute-start.3 = (f32[96,384]{1,0:T(8,128)S(1)}, f32[96,384]{1,0:T(8,128)S(1)}, u32[]{:S(2)}, u32[]{:S(2)}) collective-permute-start(f32[96,384]{1,0:T(8,128)S(1)} %get-tuple-element.71), channel_id=1, source_target_pairs={{0,1},{1,2},{2,3},{4,5},{5,6},{6,7},{8,9},{9,10},{10,11},{12,13},{... | collective-permute-start | bytes 442376 | tf_op jit(solution)/shard_map/ppermute | solution.py:56
  99.7 7.2 %collective-permute-start.2 = (f32[96,384]{1,0:T(8,128)S(1)}, f32[96,384]{1,0:T(8,128)S(1)}, u32[]{:S(2)}, u32[]{:S(2)}) collective-permute-start(f32[96,384]{1,0:T(8,128)S(1)} %get-tuple-element.71), channel_id=1, source_target_pairs={{1,0},{2,1},{3,2},{5,4},{6,5},{7,6},{9,8},{10,9},{11,10},{13,12},{... | collective-permute-start | bytes 442376 | tf_op jit(solution)/shard_map/ppermute | solution.py:56
  109.4 19.5 %all-to-all-start.6 = ((f32[16,96,128]{2,1,0:T(8,128)}), f32[16,96,128]{2,1,0:T(8,128)S(1)}, u32[]{:S(2)}, u32[]{:S(2)}) async-start(f32[16,96,128]{2,1,0:T(8,128)} %get-tuple-element.72), calls=%async_computation.6 | async-start | bytes 1572864 | tf_op jit(solution)/shard_map/all_to_all | solution.py:52
  114.8 14.0 %collective-permute-start.6 = (f32[32,256]{1,0:T(8,128)S(1)}, f32[32,256]{1,0:T(8,128)S(1)}, u32[]{:S(2)}, u32[]{:S(2)}) collective-permute-start(f32[32,256]{1,0:T(8,128)S(1)} %get-tuple-element.73), channel_id=1, source_target_pairs={{16,0},{17,1},{18,2},{19,3},{20,4},{21,5},{22,6},{23,7},{24,8},{25... | collective-permute-start | bytes 98312 | tf_op jit(solution)/shard_map/ppermute | solution.py:56
  116.1 12.7 %collective-permute-start.7 = (f32[32,256]{1,0:T(8,128)S(1)}, f32[32,256]{1,0:T(8,128)S(1)}, u32[]{:S(2)}, u32[]{:S(2)}) collective-permute-start(f32[32,256]{1,0:T(8,128)S(1)} %get-tuple-element.74), channel_id=1, source_target_pairs={{0,16},{1,17},{2,18},{3,19},{4,20},{5,21},{6,22},{7,23},{8,24},{9,... | collective-permute-start | bytes 98312 | tf_op jit(solution)/shard_map/ppermute | solution.py:56
  148.3 12.4 %all-to-all-start.8 = ((f32[16,16,128]{2,1,0:T(8,128)}), f32[16,16,128]{2,1,0:T(8,128)S(1)}, u32[]{:S(2)}, u32[]{:S(2)}) async-start(f32[16,16,128]{2,1,0:T(8,128)} %shard_map.114), calls=%async_computation.8 | async-start | bytes 262144 | tf_op jit(solution)/shard_map/all_to_all | solution.py:52
  184.0 19.7 %all-to-all-start.10 = ((f32[16,96,128]{2,1,0:T(8,128)}), f32[16,96,128]{2,1,0:T(8,128)S(1)}, u32[]{:S(2)}, u32[]{:S(2)}) async-start(f32[16,96,128]{2,1,0:T(8,128)} %get-tuple-element.87), calls=%async_computation.10 | async-start | bytes 1572864 | tf_op jit(solution)/shard_map/all_to_all | solution.py:52
  190.0 10.1 %collective-permute-start.8 = (f32[32,256]{1,0:T(8,128)S(1)}, f32[32,256]{1,0:T(8,128)S(1)}, u32[]{:S(2)}, u32[]{:S(2)}) collective-permute-start(f32[32,256]{1,0:T(8,128)S(1)} %get-tuple-element.88), channel_id=1, source_target_pairs={{16,0},{17,1},{18,2},{19,3},{20,4},{21,5},{22,6},{23,7},{24,8},{25... | collective-permute-start | bytes 98312 | tf_op jit(solution)/shard_map/ppermute | solution.py:56
  191.3 9.0 %collective-permute-start.9 = (f32[32,256]{1,0:T(8,128)S(1)}, f32[32,256]{1,0:T(8,128)S(1)}, u32[]{:S(2)}, u32[]{:S(2)}) collective-permute-start(f32[32,256]{1,0:T(8,128)S(1)} %get-tuple-element.89), channel_id=1, source_target_pairs={{0,16},{1,17},{2,18},{3,19},{4,20},{5,21},{6,22},{7,23},{8,24},{9,... | collective-permute-start | bytes 98312 | tf_op jit(solution)/shard_map/ppermute | solution.py:56

commit v4 on v3

--- a/solution.py
+++ b/solution.py
@@ -211,9 +211,9 @@
     weights = dot6(modes, rhs, 1)
     weights_ref[...] = weights
     message_ref[:, :PM, :] = jnp.zeros((GX, PM, 128), jnp.float32)
-    message_ref[:, :PM, :CASES] = jnp.broadcast_to(weights[None], (GX, PM, CASES))
+    message_ref[:, :NM, :CASES] = jnp.broadcast_to(weights[None, :NM], (GX, NM, CASES))
     for t in range(3):
-        message_ref[:, PM * (t + 1) : PM * (t + 2), :] = parcel_ref[:, :, 128 * t : 128 * (t + 1)]
+        message_ref[:, NM * (t + 1) : NM * (t + 2), :] = parcel_ref[:, :NM, 128 * t : 128 * (t + 1)]
     gram_ref[...] = dot6(modes, lifts, 1)
 
 
@@ -270,11 +270,12 @@
 
 
 def combine_first_kernel(first_ref, out_ref, coarse_ref, block_ref):
-    for t in range(3):
-        part = first_ref[:, PM * (t + 1) : PM * (t + 2), :].reshape(GX * PM, 128)
-        coarse_ref[:, 128 * t : 128 * (t + 1)] = part
+    coarse_ref[...] = jnp.zeros((GX * PM, 384), jnp.float32)
     for i in range(GX):
-        block_ref[NM * i : NM * (i + 1), :] = coarse_ref[PM * i : PM * i + NM, :]
+        for t in range(3):
+            part = first_ref[i, NM * (t + 1) : NM * (t + 2), :]
+            coarse_ref[PM * i : PM * i + NM, 128 * t : 128 * (t + 1)] = part
+            block_ref[NM * i : NM * (i + 1), 128 * t : 128 * (t + 1)] = part
     combine(first_ref[:, :PM, :], coarse_ref[...], out_ref)
 
 
@@ -535,7 +536,7 @@
             shaped(CASES, ROWS),
             shaped(SLOTS, ROWS),
             shaped(PM, CASES),
-            shaped(GX, CASES, 128),
+            shaped(GX, 4 * NM, 128),
             shaped(PM, SLOTS),
         ],
         table,

time: 209 us -> 208 us (level)
  no operation moved by 1% of the time
where the time goes in v4:
time: 208 us; the launch traced here: 206 us
  starting transfers between devices  73.2 us (35%)
  blocking collectives  58.2 us (28%)
  waiting for transfers between devices  38.8 us (19%)
  Pallas kernels  31.4 us (15%)
  local copies, waits for them, and re-layouts  3.33 us (2%)
    all_to_all x4, blocking collectives, swap(): lax.all_to_all(block, 'dom', 0, 0, tiled=True, axis_index_groups=groups)  58.2 us
    all_to_all x7, starting transfers between devices, swap(): lax.all_to_all(block, 'dom', 0, 0, tiled=True, axis_index_groups=groups)  43 us
    ppermute x10, starting transfers between devices, trade(): lax.ppermute(p, 'dom', ROUTES[d])  30.2 us
    pallas_call x13, Pallas kernels, call(): pl.pallas_call(kernel, out_shape=outs, in_specs=[SMEM] * smem + [VMEM] *...  20.8 us
    ppermute x10, waiting for transfers between devices, trade(): lax.ppermute(p, 'dom', ROUTES[d])  20.2 us
    all_to_all x7, waiting for transfers between devices, swap(): lax.all_to_all(block, 'dom', 0, 0, tiled=True, axis_index_groups=groups)  18.6 us
    pallas_call x2, Pallas kernels, schur_call(): pl.pallas_call(kernel, out_shape=outs, in_specs=[VMEM] * (len(args) - 1)...  10.7 us
  transfers between devices with their start and end apart: 17, of which 12 were waited for; matrix products, arithmetic and copies ran while one was open for 0% of the time, Pallas kernels for 4%

profile of v4, /device:TPU:1, one launch (start us, length us, event | category | flops | bytes accessed | tf_op | source)
XLA Modules:
  0.0 206.3 jit_solution(13116608980905848517)
XLA Ops:
  6.4 6.9 %all-to-all-start = ((f32[16,80,128]{2,1,0:T(8,128)}), f32[16,80,128]{2,1,0:T(8,128)S(1)}, u32[]{:S(2)}, u32[]{:S(2)}) async-start(f32[16,80,128]{2,1,0:T(8,128)} %get-tuple-element.48), calls=%async_computation | async-start | bytes 1310720 | tf_op jit(solution)/shard_map/all_to_all | solution.py:52
  14.6 5.5 %collective-permute-start.1 = (f32[40,256]{1,0:T(8,128)S(1)}, f32[40,256]{1,0:T(8,128)S(1)}, u32[]{:S(2)}, u32[]{:S(2)}) collective-permute-start(f32[40,256]{1,0:T(8,128)S(1)} %get-tuple-element.50), channel_id=1, source_target_pairs={{0,16},{1,17},{2,18},{3,19},{4,20},{5,21},{6,22},{7,23},{8,24},{9,... | collective-permute-start | bytes 122888 | tf_op jit(solution)/shard_map/ppermute | solution.py:56
  20.2 4.9 %collective-permute-done.up_ref = f32[40,256]{1,0:T(8,128)S(1)} collective-permute-done((f32[40,256]{1,0:T(8,128)S(1)}, f32[40,256]{1,0:T(8,128)S(1)}, u32[]{:S(2)}, u32[]{:S(2)}) %collective-permute-start) | collective-permute-done | bytes 40992 | tf_op jit(solution)/shard_map/ppermute | solution.py:56
  27.1 9.6 %all-to-all-start.1 = ((f32[16,24,128]{2,1,0:T(8,128)}), f32[16,24,128]{2,1,0:T(8,128)S(1)}, u32[]{:S(2)}, u32[]{:S(2)}) async-start(f32[16,24,128]{2,1,0:T(8,128)} %get-tuple-element.52), calls=%async_computation.1 | async-start | bytes 393216 | tf_op jit(solution)/shard_map/all_to_all | solution.py:52
  36.7 4.9 %shard_map.106 = (f32[32,1536]{1,0:T(8,128)S(1)}, f32[64,1536]{1,0:T(8,128)S(1)}, f32[1,1536]{1,0:T(1,128)S(1)}) custom-call(f32[32,1536]{1,0:T(8,128)S(1)} %get-tuple-element.53.rhs_ref, f32[64,1536]{1,0:T(8,128)S(1)} %get-tuple-element.54.lifts_ref, f32[1,1536]{1,0:T(1,128)S(1)} %get-tuple-element.55.sign_ref, f32[1536,1536]{1,0:T(8,128)} %schur_ref.3), custom_call_target="tpu_custom_call" | custom-call | flops 2717908992 | bytes 9437184 | tf_op jit(solution)/shard_map/pallas_call | solution.py:482
  41.6 5.6 %all-to-all-done.1.first_ref = f32[16,24,128]{2,1,0:T(8,128)S(1)} async-done(((f32[16,24,128]{2,1,0:T(8,128)}), f32[16,24,128]{2,1,0:T(8,128)S(1)}, u32[]{:S(2)}, u32[]{:S(2)}) %all-to-all-start.1) | async-done | bytes 196640 | tf_op jit(solution)/shard_map/all_to_all | solution.py:52
  47.9 13.0 %all_to_all.55.second_ref = f32[16,16,128]{2,1,0:T(8,128)S(1)} all-to-all(f32[16,16,128]{2,1,0:T(8,128)S(1)} %get-tuple-element.58), channel_id=1, replica_groups={{0,1,2,3,4,5,6,7,8,9,10,11,12,13,14,15},{16,17,18,19,20,21,22,23,24,25,..., dimensions={0} | all-to-all | bytes 262144 | tf_op jit(solution)/shard_map/all_to_all | solution.py:52
  61.1 12.1 %all_to_all.56.first_ref = f32[16,8,128]{2,1,0:T(8,128)S(1)} all-to-all(f32[16,8,128]{2,1,0:T(8,128)S(1)} %get-tuple-element.61), channel_id=1, replica_groups={{0,16,32,48,64,80,96,112,128,144,160,176,192,208,224,240},{1,17,33,49,6..., dimensions={0} | all-to-all | bytes 131072 | tf_op jit(solution)/shard_map/all_to_all | solution.py:52
  74.6 5.4 %all-to-all-start.4 = ((f32[16,16,128]{2,1,0:T(8,128)}), f32[16,16,128]{2,1,0:T(8,128)S(1)}, u32[]{:S(2)}, u32[]{:S(2)}) async-start(f32[16,16,128]{2,1,0:T(8,128)} %shard_map.109), calls=%async_computation.4 | async-start | bytes 262144 | tf_op jit(solution)/shard_map/all_to_all | solution.py:52
  80.7 5.5 %all-to-all-done.4.second_ref = f32[16,16,128]{2,1,0:T(8,128)S(1)} async-done(((f32[16,16,128]{2,1,0:T(8,128)}), f32[16,16,128]{2,1,0:T(8,128)S(1)}, u32[]{:S(2)}, u32[]{:S(2)}) %all-to-all-start.4) | async-done | bytes 131104 | tf_op jit(solution)/shard_map/all_to_all | solution.py:52
  87.9 3.5 %all-to-all-start.5 = ((f32[16,32,128]{2,1,0:T(8,128)}), f32[16,32,128]{2,1,0:T(8,128)S(1)}, u32[]{:S(2)}, u32[]{:S(2)}) async-start(f32[16,32,128]{2,1,0:T(8,128)} %get-tuple-element.69), calls=%async_computation.5 | async-start | bytes 524288 | tf_op jit(solution)/shard_map/all_to_all | solution.py:52
  91.4 2.8 %collective-permute-start.5 = (f32[96,384]{1,0:T(8,128)S(1)}, f32[96,384]{1,0:T(8,128)S(1)}, u32[]{:S(2)}, u32[]{:S(2)}) collective-permute-start(f32[96,384]{1,0:T(8,128)S(1)} %get-tuple-element.71), channel_id=1, source_target_pairs={{0,4},{1,5},{2,6},{3,7},{4,8},{5,9},{6,10},{7,11},{8,12},{9,13},{1... | collective-permute-start | bytes 442376 | tf_op jit(solution)/shard_map/ppermute | solution.py:56
  95.6 3.1 %collective-permute-start.3 = (f32[96,384]{1,0:T(8,128)S(1)}, f32[96,384]{1,0:T(8,128)S(1)}, u32[]{:S(2)}, u32[]{:S(2)}) collective-permute-start(f32[96,384]{1,0:T(8,128)S(1)} %get-tuple-element.71), channel_id=1, source_target_pairs={{0,1},{1,2},{2,3},{4,5},{5,6},{6,7},{8,9},{9,10},{10,11},{12,13},{... | collective-permute-start | bytes 442376 | tf_op jit(solution)/shard_map/ppermute | solution.py:56
  98.7 1.9 collective-permute-start.2
  100.7 1.9 collective-permute-done.4.refs_3_
  104.0 1.9 collective-permute-done.2.refs_1_
  105.9 2.5 %shard_map.112 = (f32[16,96,128]{2,1,0:T(8,128)}, f32[32,256]{1,0:T(8,128)S(1)}, f32[32,256]{1,0:T(8,128)S(1)}) custom-call(s32[5,6]{1,0:T(8,128)S(1)} %concatenate.3.table, f32[16,32,128]{2,1,0:T(8,128)S(1)} %all-to-all-done.5.first_ref, f32[32,1792]{1,0:T(8,128)S(1)} %get-tuple-element.70.image_ref.old_image_ref, ...), custom_call_target="tpu_custom_call" | custom-call | tf_op jit(solution)/shard_map/pallas_call | solution.py:471
  108.4 5.4 %all-to-all-start.6 = ((f32[16,96,128]{2,1,0:T(8,128)}), f32[16,96,128]{2,1,0:T(8,128)S(1)}, u32[]{:S(2)}, u32[]{:S(2)}) async-start(f32[16,96,128]{2,1,0:T(8,128)} %get-tuple-element.72), calls=%async_computation.6 | async-start | bytes 1572864 | tf_op jit(solution)/shard_map/all_to_all | solution.py:52
  115.2 6.1 %collective-permute-start.7 = (f32[32,256]{1,0:T(8,128)S(1)}, f32[32,256]{1,0:T(8,128)S(1)}, u32[]{:S(2)}, u32[]{:S(2)}) collective-permute-start(f32[32,256]{1,0:T(8,128)S(1)} %get-tuple-element.74), channel_id=1, source_target_pairs={{0,16},{1,17},{2,18},{3,19},{4,20},{5,21},{6,22},{7,23},{8,24},{9,... | collective-permute-start | bytes 98312 | tf_op jit(solution)/shard_map/ppermute | solution.py:56
  121.3 6.6 %collective-permute-done.6.up_ref = f32[32,256]{1,0:T(8,128)S(1)} collective-permute-done((f32[32,256]{1,0:T(8,128)S(1)}, f32[32,256]{1,0:T(8,128)S(1)}, u32[]{:S(2)}, u32[]{:S(2)}) %collective-permute-start.6) | collective-permute-done | bytes 32800 | tf_op jit(solution)/shard_map/ppermute | solution.py:56
  128.1 18.1 %all_to_all.57.first_ref = f32[16,8,128]{2,1,0:T(8,128)S(1)} all-to-all(f32[16,8,128]{2,1,0:T(8,128)S(1)} %get-tuple-element.76), channel_id=1, replica_groups={{0,16,32,48,64,80,96,112,128,144,160,176,192,208,224,240},{1,17,33,49,6..., dimensions={0} | all-to-all | bytes 131072 | tf_op jit(solution)/shard_map/all_to_all | solution.py:52
  147.4 6.2 %all-to-all-start.8 = ((f32[16,16,128]{2,1,0:T(8,128)}), f32[16,16,128]{2,1,0:T(8,128)S(1)}, u32[]{:S(2)}, u32[]{:S(2)}) async-start(f32[16,16,128]{2,1,0:T(8,128)} %shard_map.114), calls=%async_computation.8 | async-start | bytes 262144 | tf_op jit(solution)/shard_map/all_to_all | solution.py:52
  153.6 2.7 %shard_map.115 = (f32[32,32]{1,0:T(8,128)S(1)}, f32[32,32]{1,0:T(8,128)S(1)}, f32[32,1536]{1,0:T(8,128)S(1)}, f32[32,1536]{1,0:T(8,128)S(1)}) custom-call(s32[5,6]{1,0:T(8,128)S(1)} %concatenate.3.table, f32[32,128]{1,0:T(8,128)S(1)} %get-tuple-element.78.total_ref.sums_ref, f32[32,1792]{1,0:T(8,128)S(1)} %get-tuple-element.70.image_ref.old_image_ref, ...), custom_call_target="tpu_custom_call" | custom-call | tf_op jit(solution)/shard_map/pallas_call | solution.py:471
  156.3 3.5 %all-to-all-done.8.third_ref = f32[16,16,128]{2,1,0:T(8,128)S(1)} async-done(((f32[16,16,128]{2,1,0:T(8,128)}), f32[16,16,128]{2,1,0:T(8,128)S(1)}, u32[]{:S(2)}, u32[]{:S(2)}) %all-to-all-start.8) | async-done | bytes 131104 | tf_op jit(solution)/shard_map/all_to_all | solution.py:52
  159.8 5.7 %shard_map.116 = (f32[32,1792]{1,0:T(8,128)S(1)}, f32[16,32,128]{2,1,0:T(8,128)S(1)}) custom-call(f32[16,16,128]{2,1,0:T(8,128)S(1)} %all-to-all-done.8.third_ref, f32[32,128]{1,0:T(8,128)S(1)} %get-tuple-element.77.before_ref, f32[32,32]{1,0:T(8,128)S(1)} %get-tuple-element.82.step_ref, f32[32,1536]{1,0:T(8,128)S(1)} %get-tuple-element.83.residual_ref, ...), custom_call_target="tpu_custom_call" | custom-call | flops 905969664 | bytes 9437184 | tf_op jit(solution)/shard_map/pallas_call | solution.py:482
  165.6 15.0 %all_to_all.58.first_ref = f32[16,32,128]{2,1,0:T(8,128)S(1)} all-to-all(f32[16,32,128]{2,1,0:T(8,128)S(1)} %get-tuple-element.86), channel_id=1, replica_groups={{0,16,32,48,64,80,96,112,128,144,160,176,192,208,224,240},{1,17,33,49,6..., dimensions={0} | all-to-all | bytes 524288 | tf_op jit(solution)/shard_map/all_to_all | solution.py:52
  180.5 2.5 %shard_map.117 = (f32[16,96,128]{2,1,0:T(8,128)}, f32[32,256]{1,0:T(8,128)S(1)}, f32[32,256]{1,0:T(8,128)S(1)}) custom-call(s32[5,6]{1,0:T(8,128)S(1)} %concatenate.3.table, f32[16,32,128]{2,1,0:T(8,128)S(1)} %all_to_all.58.first_ref, f32[32,1792]{1,0:T(8,128)S(1)} %get-tuple-element.85.image_ref, f32[128,384]{1,0:T(8,128)S(1)} %get-tuple-element.62.coarse_ref.refs_0_, ...), custom_call_target="tpu_custom_call" | custom-call | tf_op jit(solution)/shard_map/pallas_call | solution.py:471
  183.1 5.9 %all-to-all-start.10 = ((f32[16,96,128]{2,1,0:T(8,128)}), f32[16,96,128]{2,1,0:T(8,128)S(1)}, u32[]{:S(2)}, u32[]{:S(2)}) async-start(f32[16,96,128]{2,1,0:T(8,128)} %get-tuple-element.87), calls=%async_computation.10 | async-start | bytes 1572864 | tf_op jit(solution)/shard_map/all_to_all | solution.py:52
  190.3 5.5 %collective-permute-start.9 = (f32[32,256]{1,0:T(8,128)S(1)}, f32[32,256]{1,0:T(8,128)S(1)}, u32[]{:S(2)}, u32[]{:S(2)}) collective-permute-start(f32[32,256]{1,0:T(8,128)S(1)} %get-tuple-element.89), channel_id=1, source_target_pairs={{0,16},{1,17},{2,18},{3,19},{4,20},{5,21},{6,22},{7,23},{8,24},{9,... | collective-permute-start | bytes 98312 | tf_op jit(solution)/shard_map/ppermute | solution.py:56
  195.8 3.3 %collective-permute-done.8.up_ref = f32[32,256]{1,0:T(8,128)S(1)} collective-permute-done((f32[32,256]{1,0:T(8,128)S(1)}, f32[32,256]{1,0:T(8,128)S(1)}, u32[]{:S(2)}, u32[]{:S(2)}) %collective-permute-start.8) | collective-permute-done | bytes 32800 | tf_op jit(solution)/shard_map/ppermute | solution.py:56
  199.3 3.5 %all-to-all-done.10.second_ref = f32[16,96,128]{2,1,0:T(8,128)S(1)} async-done(((f32[16,96,128]{2,1,0:T(8,128)}), f32[16,96,128]{2,1,0:T(8,128)S(1)}, u32[]{:S(2)}, u32[]{:S(2)}) %all-to-all-start.10) | async-done | bytes 786464 | tf_op jit(solution)/shard_map/all_to_all | solution.py:52
  202.8 3.6 %shard_map.118 = (f32[32,1536]{1,0:T(8,128)}, f32[32,1536]{1,0:T(8,128)}) custom-call(s32[5,6]{1,0:T(8,128)S(1)} %concatenate.3.table, f32[32,1792]{1,0:T(8,128)S(1)} %get-tuple-element.85.image_ref, f32[16,96,128]{2,1,0:T(8,128)S(1)} %all-to-all-done.10.second_ref, f32[32,256]{1,0:T(8,128)S(1)} %collective-permute-done.8.up_ref, ...), custom_call_target="tpu_custom_call" | custom-call | tf_op jit(solution)/shard_map/pallas_call | solution.py:471
  (29 shorter events, 20.0 us)
Async XLA Ops:
  2.1 0.9 copy-start
  3.0 0.8 copy-start.1
  3.8 0.8 copy-start.2
  6.4 19.0 %all-to-all-start = ((f32[16,80,128]{2,1,0:T(8,128)}), f32[16,80,128]{2,1,0:T(8,128)S(1)}, u32[]{:S(2)}, u32[]{:S(2)}) async-start(f32[16,80,128]{2,1,0:T(8,128)} %get-tuple-element.48), calls=%async_computation | async-start | bytes 1310720 | tf_op jit(solution)/shard_map/all_to_all | solution.py:52
  13.4 11.7 %collective-permute-start = (f32[40,256]{1,0:T(8,128)S(1)}, f32[40,256]{1,0:T(8,128)S(1)}, u32[]{:S(2)}, u32[]{:S(2)}) collective-permute-start(f32[40,256]{1,0:T(8,128)S(1)} %get-tuple-element.49), channel_id=1, source_target_pairs={{16,0},{17,1},{18,2},{19,3},{20,4},{21,5},{22,6},{23,7},{24,8},{25... | collective-permute-start | bytes 122888 | tf_op jit(solution)/shard_map/ppermute | solution.py:56
  14.6 10.4 %collective-permute-start.1 = (f32[40,256]{1,0:T(8,128)S(1)}, f32[40,256]{1,0:T(8,128)S(1)}, u32[]{:S(2)}, u32[]{:S(2)}) collective-permute-start(f32[40,256]{1,0:T(8,128)S(1)} %get-tuple-element.50), channel_id=1, source_target_pairs={{0,16},{1,17},{2,18},{3,19},{4,20},{5,21},{6,22},{7,23},{8,24},{9,... | collective-permute-start | bytes 122888 | tf_op jit(solution)/shard_map/ppermute | solution.py:56
  27.1 20.2 %all-to-all-start.1 = ((f32[16,24,128]{2,1,0:T(8,128)}), f32[16,24,128]{2,1,0:T(8,128)S(1)}, u32[]{:S(2)}, u32[]{:S(2)}) async-start(f32[16,24,128]{2,1,0:T(8,128)} %get-tuple-element.52), calls=%async_computation.1 | async-start | bytes 393216 | tf_op jit(solution)/shard_map/all_to_all | solution.py:52
  74.6 11.6 %all-to-all-start.4 = ((f32[16,16,128]{2,1,0:T(8,128)}), f32[16,16,128]{2,1,0:T(8,128)S(1)}, u32[]{:S(2)}, u32[]{:S(2)}) async-start(f32[16,16,128]{2,1,0:T(8,128)} %shard_map.109), calls=%async_computation.4 | async-start | bytes 262144 | tf_op jit(solution)/shard_map/all_to_all | solution.py:52
  87.9 18.0 %all-to-all-start.5 = ((f32[16,32,128]{2,1,0:T(8,128)}), f32[16,32,128]{2,1,0:T(8,128)S(1)}, u32[]{:S(2)}, u32[]{:S(2)}) async-start(f32[16,32,128]{2,1,0:T(8,128)} %get-tuple-element.69), calls=%async_computation.5 | async-start | bytes 524288 | tf_op jit(solution)/shard_map/all_to_all | solution.py:52
  91.4 9.2 %collective-permute-start.5 = (f32[96,384]{1,0:T(8,128)S(1)}, f32[96,384]{1,0:T(8,128)S(1)}, u32[]{:S(2)}, u32[]{:S(2)}) collective-permute-start(f32[96,384]{1,0:T(8,128)S(1)} %get-tuple-element.71), channel_id=1, source_target_pairs={{0,4},{1,5},{2,6},{3,7},{4,8},{5,9},{6,10},{7,11},{8,12},{9,13},{1... | collective-permute-start | bytes 442376 | tf_op jit(solution)/shard_map/ppermute | solution.py:56
  94.3 8.2 %collective-permute-start.4 = (f32[96,384]{1,0:T(8,128)S(1)}, f32[96,384]{1,0:T(8,128)S(1)}, u32[]{:S(2)}, u32[]{:S(2)}) collective-permute-start(f32[96,384]{1,0:T(8,128)S(1)} %get-tuple-element.71), channel_id=1, source_target_pairs={{4,0},{5,1},{6,2},{7,3},{8,4},{9,5},{10,6},{11,7},{12,8},{13,9},{1... | collective-permute-start | bytes 442376 | tf_op jit(solution)/shard_map/ppermute | solution.py:56
  95.6 8.4 %collective-permute-start.3 = (f32[96,384]{1,0:T(8,128)S(1)}, f32[96,384]{1,0:T(8,128)S(1)}, u32[]{:S(2)}, u32[]{:S(2)}) collective-permute-start(f32[96,384]{1,0:T(8,128)S(1)} %get-tuple-element.71), channel_id=1, source_target_pairs={{0,1},{1,2},{2,3},{4,5},{5,6},{6,7},{8,9},{9,10},{10,11},{12,13},{... | collective-permute-start | bytes 442376 | tf_op jit(solution)/shard_map/ppermute | solution.py:56
  98.7 7.2 %collective-permute-start.2 = (f32[96,384]{1,0:T(8,128)S(1)}, f32[96,384]{1,0:T(8,128)S(1)}, u32[]{:S(2)}, u32[]{:S(2)}) collective-permute-start(f32[96,384]{1,0:T(8,128)S(1)} %get-tuple-element.71), channel_id=1, source_target_pairs={{1,0},{2,1},{3,2},{5,4},{6,5},{7,6},{9,8},{10,9},{11,10},{13,12},{... | collective-permute-start | bytes 442376 | tf_op jit(solution)/shard_map/ppermute | solution.py:56
  108.4 19.5 %all-to-all-start.6 = ((f32[16,96,128]{2,1,0:T(8,128)}), f32[16,96,128]{2,1,0:T(8,128)S(1)}, u32[]{:S(2)}, u32[]{:S(2)}) async-start(f32[16,96,128]{2,1,0:T(8,128)} %get-tuple-element.72), calls=%async_computation.6 | async-start | bytes 1572864 | tf_op jit(solution)/shard_map/all_to_all | solution.py:52
  113.9 14.0 %collective-permute-start.6 = (f32[32,256]{1,0:T(8,128)S(1)}, f32[32,256]{1,0:T(8,128)S(1)}, u32[]{:S(2)}, u32[]{:S(2)}) collective-permute-start(f32[32,256]{1,0:T(8,128)S(1)} %get-tuple-element.73), channel_id=1, source_target_pairs={{16,0},{17,1},{18,2},{19,3},{20,4},{21,5},{22,6},{23,7},{24,8},{25... | collective-permute-start | bytes 98312 | tf_op jit(solution)/shard_map/ppermute | solution.py:56
  115.2 12.7 %collective-permute-start.7 = (f32[32,256]{1,0:T(8,128)S(1)}, f32[32,256]{1,0:T(8,128)S(1)}, u32[]{:S(2)}, u32[]{:S(2)}) collective-permute-start(f32[32,256]{1,0:T(8,128)S(1)} %get-tuple-element.74), channel_id=1, source_target_pairs={{0,16},{1,17},{2,18},{3,19},{4,20},{5,21},{6,22},{7,23},{8,24},{9,... | collective-permute-start | bytes 98312 | tf_op jit(solution)/shard_map/ppermute | solution.py:56
  147.4 12.4 %all-to-all-start.8 = ((f32[16,16,128]{2,1,0:T(8,128)}), f32[16,16,128]{2,1,0:T(8,128)S(1)}, u32[]{:S(2)}, u32[]{:S(2)}) async-start(f32[16,16,128]{2,1,0:T(8,128)} %shard_map.114), calls=%async_computation.8 | async-start | bytes 262144 | tf_op jit(solution)/shard_map/all_to_all | solution.py:52
  183.1 19.7 %all-to-all-start.10 = ((f32[16,96,128]{2,1,0:T(8,128)}), f32[16,96,128]{2,1,0:T(8,128)S(1)}, u32[]{:S(2)}, u32[]{:S(2)}) async-start(f32[16,96,128]{2,1,0:T(8,128)} %get-tuple-element.87), calls=%async_computation.10 | async-start | bytes 1572864 | tf_op jit(solution)/shard_map/all_to_all | solution.py:52
  189.0 10.1 %collective-permute-start.8 = (f32[32,256]{1,0:T(8,128)S(1)}, f32[32,256]{1,0:T(8,128)S(1)}, u32[]{:S(2)}, u32[]{:S(2)}) collective-permute-start(f32[32,256]{1,0:T(8,128)S(1)} %get-tuple-element.88), channel_id=1, source_target_pairs={{16,0},{17,1},{18,2},{19,3},{20,4},{21,5},{22,6},{23,7},{24,8},{25... | collective-permute-start | bytes 98312 | tf_op jit(solution)/shard_map/ppermute | solution.py:56
  190.3 9.0 %collective-permute-start.9 = (f32[32,256]{1,0:T(8,128)S(1)}, f32[32,256]{1,0:T(8,128)S(1)}, u32[]{:S(2)}, u32[]{:S(2)}) collective-permute-start(f32[32,256]{1,0:T(8,128)S(1)} %get-tuple-element.89), channel_id=1, source_target_pairs={{0,16},{1,17},{2,18},{3,19},{4,20},{5,21},{6,22},{7,23},{8,24},{9,... | collective-permute-start | bytes 98312 | tf_op jit(solution)/shard_map/ppermute | solution.py:56
